TPU v7x, 32 devices: a whole 2x2x4 slice. The times are simulated.
32 devices in a mesh: dp: 4 (over z), row: 4 (over x, core), col: 2 (over y).
Axes of the slice: x: 2, y: 2, z: 4, core: 2. Of those that a mesh axis runs over, the one named last changes fastest.
Arguments:
- hidden_in: bfloat16 [8192, 1536], P(('dp', 'row', 'col')), may hold values from -6 to 6
- lengths: int32 [16], replicated, may hold values from 1 to 1024, as said below
- perm: int32 [16], P('dp'), may hold values from 0 to 15, as said below
- norm_gain: float32 [1536], replicated, may hold values from 0.5 to 1.5
- w_z: float32 [1536, 3072], P('dp', ('row', 'col')), may hold values from -0.15625 to 0.15625
- w_x: float32 [1536, 3072], P('dp', ('row', 'col')), may hold values from -0.15625 to 0.15625
- w_dt: float32 [1536, 48], P('dp', ('row', 'col')), may hold values from -0.15625 to 0.15625
- w_bc: float32 [1536, 256], P('dp'), may hold values from -0.15625 to 0.15625
- conv_x: float32 [4, 3072], replicated, may hold values from -3 to 3
- conv_x_bias: float32 [3072], replicated, may hold values from -3 to 3
- conv_bc: float32 [4, 256], replicated, may hold values from -3 to 3
- conv_bc_bias: float32 [256], replicated, may hold values from -3 to 3
- dt_bias: float32 [48], replicated, may hold values from -7 to -3
- a_log: float32 [48], replicated, may hold values from 0 to 2.77
- skip_d: float32 [48], replicated, may hold values from 0.5 to 1.5
- gate_gain: float32 [3072], replicated, may hold values from 0.5 to 1.5
- w_out: float32 [3072, 1536], P(('row', 'col'), 'dp'), may hold values from -0.109375 to 0.109375
- grad_out: bfloat16 [8192, 1536], P(('dp', 'row', 'col')), may hold values from -6 to 6
Outputs:
- block_out: bfloat16 [8192, 1536], P(('dp', 'row', 'col'))
- grad_in: bfloat16 [8192, 1536], P(('dp', 'row', 'col'))
- g_norm_gain: float32 [1536], replicated
- g_w_z: float32 [1536, 3072], P('dp', ('row', 'col'))
- g_w_x: float32 [1536, 3072], P('dp', ('row', 'col'))
- g_w_dt: float32 [1536, 48], P('dp', ('row', 'col'))
- g_w_bc: float32 [1536, 256], P('dp')
- g_conv_x: float32 [4, 3072], replicated
- g_conv_x_bias: float32 [3072], replicated
- g_conv_bc: float32 [4, 256], replicated
- g_conv_bc_bias: float32 [256], replicated
- g_dt_bias: float32 [48], replicated
- g_a_log: float32 [48], replicated
- g_skip_d: float32 [48], replicated
- g_gate_gain: float32 [3072], replicated
- g_w_out: float32 [3072, 1536], P(('row', 'col'), 'dp')
Inputs may be any that keep to these rules, and one draw needn't show every extreme that they name: In every group the 4 lengths of its slots sum to 2048, and the longest of them is exactly 1024. `perm`: A permutation of the sequences.
All inputs are finite; a program needn't handle non-finite values.
Results may differ from a plain program's by a relative error of at most 0.012.
Values may be sent and summed in bfloat16 or wider, within the bound.
A program may use at most 192 MiB of HBM per device.

v0:
```python
import jax
import jax.numpy as jnp
from jax import lax
from jax.sharding import PartitionSpec as P

SPAN = 256
INNER = 3072


EPSILON = 1e-05
HIGHEST = lax.Precision.HIGHEST


def norm_in(inputs, gains):
    return inputs * lax.rsqrt(jnp.mean(inputs * inputs, axis=-1, keepdims=True) + EPSILON) * gains


def dealt_lengths(lengths, slot_ids):
    seq_ids = jnp.arange(lengths.shape[0], dtype=jnp.int32)
    return jnp.sum(jnp.where(slot_ids[:, None] == seq_ids[None, :], lengths[None, :], 0), axis=1)


def token_layout(dealt_len, length):
    offsets = jnp.cumsum(dealt_len) - dealt_len
    positions = jnp.arange(length, dtype=jnp.int32)
    starts = jnp.sum((positions[:, None] == offsets[None, :]).astype(jnp.int32), axis=1)
    begin_at = jnp.max(
        jnp.where(offsets[None, :] <= positions[:, None], offsets[None, :], 0), axis=1
    )
    return (starts, positions - begin_at)


def causal_conv(values, kernel, offset, places):
    n_taps = kernel.shape[0]
    result = kernel[n_taps - 1] * values + offset
    for back_by in range(1, n_taps):
        shifted = jnp.concatenate(
            [jnp.zeros((back_by, values.shape[1]), values.dtype), values[:-back_by]], axis=0
        )
        result = result + kernel[n_taps - 1 - back_by] * jnp.where(
            (places >= back_by)[:, None], shifted, 0.0
        )
    return result


def ssd_scan(x_heads, dt_soft, decay_rate, b_mat, c_mat, starts):
    length, n_heads, head_dim = x_heads.shape
    n_state = b_mat.shape[1]
    n_blocks = length // SPAN
    blocks = (
        x_heads.reshape(n_blocks, SPAN, n_heads, head_dim),
        dt_soft.reshape(n_blocks, SPAN, n_heads),
        b_mat.reshape(n_blocks, SPAN, n_state),
        c_mat.reshape(n_blocks, SPAN, n_state),
        starts.reshape(n_blocks, SPAN),
    )
    positions = jnp.arange(SPAN, dtype=jnp.int32)
    lower_mask = positions[:, None] >= positions[None, :]

    def advance(hidden, block_data):
        x_block, dt_block, b_block, c_block, f_block = block_data
        log_decay = jnp.cumsum(dt_block * decay_rate[None, :], axis=0)
        segment = jnp.cumsum(f_block)
        same_seq = (segment[:, None] == segment[None, :]) & lower_mask
        decays = jnp.exp(
            jnp.where(same_seq[:, :, None], log_decay[:, None, :] - log_decay[None, :, :], -1e30)
        )
        gram_mat = jnp.dot(c_block, b_block.T, precision=HIGHEST)
        mixing = decays * gram_mat[:, :, None] * dt_block[None, :, :]
        inside = jnp.einsum("ijh,jhp->ihp", mixing, x_block, precision=HIGHEST)
        carried = (
            jnp.einsum("in,hpn->ihp", c_block, hidden, precision=HIGHEST)
            * jnp.exp(log_decay)[:, :, None]
        )
        carried = jnp.where((segment == 0)[:, None, None], carried, 0.0)
        last_mark = segment[-1]
        end_weight = (
            jnp.where(
                (segment == last_mark)[:, None], jnp.exp(log_decay[-1][None, :] - log_decay), 0.0
            )
            * dt_block
        )
        fresh_state = jnp.einsum("jh,jhp,jn->hpn", end_weight, x_block, b_block, precision=HIGHEST)
        kept_share = jnp.where(last_mark == 0, jnp.exp(log_decay[-1]), 0.0)
        return (fresh_state + kept_share[:, None, None] * hidden, inside + carried)

    zero_state = jnp.zeros((n_heads, head_dim, n_state), x_heads.dtype)
    _, outputs = lax.scan(jax.checkpoint(advance), zero_state, blocks)
    return outputs.reshape(length, n_heads, head_dim)


def mixer(
    z_raw,
    x_raw,
    dt_raw,
    bc_raw,
    conv_x,
    conv_x_bias,
    conv_bc,
    conv_bc_bias,
    dt_bias,
    a_log,
    skip_d,
    starts,
    places,
):
    n_heads = dt_bias.shape[0]
    n_state = bc_raw.shape[1] // 2
    length = x_raw.shape[0]
    x_conv = jax.nn.silu(causal_conv(x_raw, conv_x, conv_x_bias, places))
    bc_conv = jax.nn.silu(causal_conv(bc_raw, conv_bc, conv_bc_bias, places))
    dt_soft = jax.nn.softplus(dt_raw + dt_bias)
    x_heads = x_conv.reshape(length, n_heads, -1)
    scanned = ssd_scan(
        x_heads, dt_soft, -jnp.exp(a_log), bc_conv[:, :n_state], bc_conv[:, n_state:], starts
    )
    outputs = scanned + skip_d[None, :, None] * x_heads
    return outputs.reshape(length, -1) * jax.nn.silu(z_raw)


def shards(
    hidden_in,
    lengths,
    perm,
    norm_gain,
    w_z,
    w_x,
    w_dt,
    w_bc,
    conv_x,
    conv_x_bias,
    conv_bc,
    conv_bc_bias,
    dt_bias,
    a_log,
    skip_d,
    gate_gain,
    w_out,
    grad_out,
):
    grid_size = lax.axis_size("row") * lax.axis_size("col")
    place_index = lax.axis_index("row") * lax.axis_size("col") + lax.axis_index("col")
    tok_rows = hidden_in.shape[0]
    tok_group = tok_rows * grid_size
    inner_part = w_z.shape[1]
    heads_part = w_dt.shape[1]
    inner_first = place_index * inner_part
    heads_first = place_index * heads_part
    contract_last = (((1,), (1,)), ((), ()))
    contract_first = (((0,), (0,)), ((), ()))
    inputs = hidden_in.astype(jnp.float32)
    normed, norm_pull = jax.vjp(norm_in, inputs, norm_gain)
    normed_low = normed.astype(jnp.bfloat16)
    masters = (
        w_z.astype(jnp.bfloat16),
        w_x.astype(jnp.bfloat16),
        w_dt.astype(jnp.bfloat16),
        w_bc.astype(jnp.bfloat16),
        w_out.astype(jnp.bfloat16),
    )
    gathered = (
        lax.all_gather(masters[0], "dp", axis=0, tiled=True),
        lax.all_gather(masters[1], "dp", axis=0, tiled=True),
        lax.all_gather(masters[2], "dp", axis=0, tiled=True),
        lax.all_gather(masters[3], "dp", axis=0, tiled=True),
        lax.all_gather(masters[4], "dp", axis=1, tiled=True),
    )
    in_weight = jnp.concatenate([gathered[0], gathered[1], gathered[2]], axis=1)
    bc_weight = gathered[3]
    out_weight = gathered[4]
    rows_all = lax.all_gather(normed_low, ("row", "col"), axis=0, tiled=True)
    projected = jnp.dot(rows_all, in_weight, preferred_element_type=jnp.float32)
    bc_raw = jnp.dot(rows_all, bc_weight, preferred_element_type=jnp.float32)
    starts, places = token_layout(dealt_lengths(lengths, perm), tok_group)
    conv_x_part = lax.dynamic_slice_in_dim(conv_x, inner_first, inner_part, 1)
    conv_xb_part = lax.dynamic_slice_in_dim(conv_x_bias, inner_first, inner_part, 0)
    dt_bias_part = lax.dynamic_slice_in_dim(dt_bias, heads_first, heads_part, 0)
    a_log_part = lax.dynamic_slice_in_dim(a_log, heads_first, heads_part, 0)
    skip_part = lax.dynamic_slice_in_dim(skip_d, heads_first, heads_part, 0)
    gain_part = lax.dynamic_slice_in_dim(gate_gain, inner_first, inner_part, 0)

    def local_mixer(
        proj_rows, bc_rows, taps_x, bias_x, taps_bc, bias_bc, step_bias, rate_log, skip_heads
    ):
        return mixer(
            proj_rows[:, :inner_part],
            proj_rows[:, inner_part : 2 * inner_part],
            proj_rows[:, 2 * inner_part :],
            bc_rows,
            taps_x,
            bias_x,
            taps_bc,
            bias_bc,
            step_bias,
            rate_log,
            skip_heads,
            starts,
            places,
        )

    gated_rows, mixer_pull = jax.vjp(
        local_mixer,
        projected,
        bc_raw,
        conv_x_part,
        conv_xb_part,
        conv_bc,
        conv_bc_bias,
        dt_bias_part,
        a_log_part,
        skip_part,
    )
    square_sum = lax.psum(jnp.sum(gated_rows * gated_rows, axis=1), ("row", "col"))
    row_scale = lax.rsqrt(square_sum / INNER + EPSILON)
    normed_out = (gated_rows * row_scale[:, None] * gain_part).astype(jnp.bfloat16)
    row_block = normed_out
    mixed_out = lax.psum_scatter(
        jnp.dot(row_block, out_weight, preferred_element_type=jnp.float32).astype(jnp.bfloat16),
        ("row", "col"),
        scatter_dimension=0,
        tiled=True,
    ).astype(jnp.float32)
    block_out = (inputs + mixed_out).astype(jnp.bfloat16)
    shard_rows = lax.all_gather(grad_out, ("row", "col"), axis=0, tiled=True)
    block_grad = lax.dot_general(
        shard_rows, out_weight, contract_last, preferred_element_type=jnp.float32
    )
    grad_weight = lax.dot_general(
        normed_out, shard_rows, contract_first, preferred_element_type=jnp.float32
    )
    weighted = block_grad * gain_part
    cross_sum = lax.psum(jnp.sum(weighted * gated_rows, axis=1), ("row", "col"))
    grad_gated = (
        row_scale[:, None] * weighted
        - gated_rows * (row_scale * row_scale * row_scale * cross_sum / INNER)[:, None]
    )
    grad_gain_part = jnp.sum(block_grad * gated_rows * row_scale[:, None], axis=0)
    pulled = mixer_pull(grad_gated)
    grad_bc = lax.psum(pulled[1], ("row", "col"))
    projected_low = pulled[0].astype(jnp.bfloat16)
    bc_low = grad_bc.astype(jnp.bfloat16)
    row_block = projected_low
    grad_normed_in = lax.psum_scatter(
        lax.dot_general(row_block, in_weight, contract_last, preferred_element_type=jnp.float32),
        ("row", "col"),
        scatter_dimension=0,
        tiled=True,
    )
    own_bc = lax.dynamic_slice_in_dim(bc_low, place_index * tok_rows, tok_rows, 0)
    grad_normed_in = grad_normed_in + lax.dot_general(
        own_bc, bc_weight, contract_last, preferred_element_type=jnp.float32
    )
    grad_in_weight = lax.dot_general(
        rows_all, projected_low, contract_first, preferred_element_type=jnp.float32
    )
    grad_bc_weight = lax.dot_general(
        rows_all, bc_low, contract_first, preferred_element_type=jnp.float32
    )
    reduced = (
        lax.psum_scatter(
            grad_in_weight[:, :inner_part].astype(jnp.bfloat16),
            "dp",
            scatter_dimension=0,
            tiled=True,
        ).astype(jnp.float32),
        lax.psum_scatter(
            grad_in_weight[:, inner_part : 2 * inner_part].astype(jnp.bfloat16),
            "dp",
            scatter_dimension=0,
            tiled=True,
        ).astype(jnp.float32),
        lax.psum_scatter(
            grad_in_weight[:, 2 * inner_part :].astype(jnp.bfloat16),
            "dp",
            scatter_dimension=0,
            tiled=True,
        ).astype(jnp.float32),
        lax.psum_scatter(
            grad_bc_weight.astype(jnp.bfloat16), "dp", scatter_dimension=0, tiled=True
        ).astype(jnp.float32),
        lax.psum_scatter(
            grad_weight.astype(jnp.bfloat16), "dp", scatter_dimension=1, tiled=True
        ).astype(jnp.float32),
    )
    grad_inputs, grad_norm_gain = norm_pull(grad_normed_in)
    grad_in = (grad_out.astype(jnp.float32) + grad_inputs).astype(jnp.bfloat16)
    conv_x_grad = lax.dynamic_update_slice_in_dim(jnp.zeros_like(conv_x), pulled[2], inner_first, 1)
    conv_xb_grad = lax.dynamic_update_slice_in_dim(
        jnp.zeros_like(conv_x_bias), pulled[3], inner_first, 0
    )
    dt_bias_grad = lax.dynamic_update_slice_in_dim(
        jnp.zeros_like(dt_bias), pulled[6], heads_first, 0
    )
    a_log_grad = lax.dynamic_update_slice_in_dim(jnp.zeros_like(a_log), pulled[7], heads_first, 0)
    skip_grad = lax.dynamic_update_slice_in_dim(jnp.zeros_like(skip_d), pulled[8], heads_first, 0)
    gain_grad = lax.dynamic_update_slice_in_dim(
        jnp.zeros_like(gate_gain), grad_gain_part, inner_first, 0
    )
    small_sums = lax.psum(
        (
            grad_norm_gain,
            conv_x_grad,
            conv_xb_grad,
            pulled[4],
            pulled[5],
            dt_bias_grad,
            a_log_grad,
            skip_grad,
            gain_grad,
        ),
        ("dp", "row", "col"),
    )
    return (
        block_out,
        grad_in,
        small_sums[0],
        reduced[0],
        reduced[1],
        reduced[2],
        reduced[3],
        small_sums[1],
        small_sums[2],
        small_sums[3],
        small_sums[4],
        small_sums[5],
        small_sums[6],
        small_sums[7],
        small_sums[8],
        reduced[4],
    )


def solution(mesh):
    return jax.shard_map(
        shards,
        mesh=mesh,
        in_specs=(
            P(("dp", "row", "col"), None),
            P(),
            P("dp"),
            P(),
            P("dp", ("row", "col")),
            P("dp", ("row", "col")),
            P("dp", ("row", "col")),
            P("dp", None),
            P(),
            P(),
            P(),
            P(),
            P(),
            P(),
            P(),
            P(),
            P(("row", "col"), "dp"),
            P(("dp", "row", "col"), None),
        ),
        out_specs=(
            P(("dp", "row", "col"), None),
            P(("dp", "row", "col"), None),
            P(),
            P("dp", ("row", "col")),
            P("dp", ("row", "col")),
            P("dp", ("row", "col")),
            P("dp", None),
            P(),
            P(),
            P(),
            P(),
            P(),
            P(),
            P(),
            P(),
            P(("row", "col"), "dp"),
        ),
        check_vma=False,
    )
```

profile of v0, /device:TPU:8, one launch (start us, length us, event | category | flops | bytes accessed | tf_op | source)
XLA Modules:
  0.0 1551.6 jit_solution(11034230062325643612)
XLA Ops:
  22.1 13.5 all_gather.24
  35.9 18.6 %all_gather.25 = bf16[1536,256]{1,0:T(8,128)(2,1)S(1)} all-gather(bf16[384,256]{1,0:T(8,128)(2,1)S(1)} %convert_element_type.78), channel_id=1, replica_groups=mesh['dp'=4,'row'=4,'col'=2] {'dp'}, dimensions={0}, use_global_device_ids=true | all-gather | bytes 983040 | tf_op jit(solution)/shard_map/all_gather | solution.py:165
  55.6 21.8 %all-gather.10.cloned.1.call-done = bf16[1536,384]{1,0:T(8,128)(2,1)} async-done(((bf16[384,384]{1,0:T(8,128)(2,1)}), bf16[1536,384]{1,0:T(8,128)(2,1)}) %all-gather.10.cloned.1.call-update) | async-done | bytes 1179664 | tf_op jit(solution)/shard_map/all_gather | solution.py:163
  77.4 47.6 %all-gather.6.cloned.1.call-done = bf16[2048,1536]{1,0:T(8,128)(2,1)} async-done(((bf16[256,1536]{1,0:T(8,128)(2,1)}), bf16[2048,1536]{1,0:T(8,128)(2,1)}) %all-gather.6.cloned.1.call-update) | async-done | bytes 6291472 | tf_op jit(solution)/shard_map/all_gather | solution.py:171
  158.6 199.3 %while.41 = (s32[]{:T(128)}, f32[6,64,128]{2,1,0:T(8,128)S(1)}, f32[8,256,6,64]{1,0,3,2:T(8,128)}, f32[8,6,64,128]{3,2,1,0:T(8,128)}, s32[8,256]{1,0:T(8,128)}, ...) while((s32[]{:T(128)}, f32[6,64,128]{2,1,0:T(8,128)S(1)}, ...), condition=%wide.region_10.11_spmd.clone, body=%wide.region_5.10_spmd.clone.sunk | while | flops 707287552 | bytes 5843418 | solution.py:88
  174.2 9.9 dynamic_update_slice.93
  199.0 9.9 dynamic_update_slice.93
  223.9 9.9 dynamic_update_slice.93
  248.8 9.9 dynamic_update_slice.93
  273.6 9.9 dynamic_update_slice.93
  298.4 9.9 dynamic_update_slice.93
  323.3 9.9 dynamic_update_slice.93
  348.1 9.9 dynamic_update_slice.93
  367.1 13.4 psum.84
  389.8 13.4 psum.85
  419.9 543.5 %while.42 = (s32[]{:T(128)}, f32[6]{0:T(128)}, f32[6,64,128]{2,1,0:T(8,128)}, f32[8,256,6,64]{1,0,3,2:T(8,128)}, f32[8,256,6]{1,2,0:T(8,128)}, /*index=5*/f32[8,...) while((s32[]{:T(128)}, f32[6]{0:T(128)}, ...), condition=%wide.region_31.32_spmd.clone, body=%wide.region_16.31_spmd.clone.sunk | while | flops 1669712896 | bytes 15386007 | solution.py:88
  996.2 88.3 %all-reduce.32 = bf16[2048,256]{1,0:T(8,128)(2,1)} all-reduce(f32[2048,256]{1,0:T(8,128)} %multiply_add_fusion.3), channel_id=1, replica_groups=mesh['dp'=4,'row'=4,'col'=2] {'row','col'}, use_global_device_ids=true, to_apply=%region_33.34 | all-reduce | flops 524288 | bytes 3145728 | tf_op jit(solution)/shard_map/psum | solution.py:239
  1123.9 13.4 fusion.129
  1151.0 25.2 %reduce-scatter.28.cloned.1.call-done = bf16[384,384]{1,0:T(8,128)(2,1)} async-done(((bf16[1536,384]{1,0:T(8,128)(2,1)}), bf16[384,384]{1,0:T(8,128)(2,1)}) %reduce-scatter.28.cloned.1.call-update) | async-done | bytes 294928
  1178.2 28.3 %reduce-scatter.24.cloned.1.call-done = bf16[384,384]{1,0:T(8,128)(2,1)} async-done(((bf16[1536,384]{1,0:T(8,128)(2,1)}), bf16[384,384]{1,0:T(8,128)(2,1)}) %reduce-scatter.24.cloned.1.call-update) | async-done | bytes 294928
  1208.7 28.0 %reduce-scatter.22.cloned.1.call-done = bf16[384,384]{1,0:T(8,128)(2,1)} async-done(((bf16[1536,384]{1,0:T(8,128)(2,1)}), bf16[384,384]{1,0:T(8,128)(2,1)}) %reduce-scatter.22.cloned.1.call-update) | async-done | bytes 294928
  1238.9 94.9 %reduce-scatter.18.cloned.1.call-done = f32[256,1536]{1,0:T(8,128)} async-done(((f32[2048,1536]{1,0:T(8,128)}), f32[256,1536]{1,0:T(8,128)}) %reduce-scatter.18.cloned.1.call-update) | async-done | bytes 1572880 | tf_op jit(solution)/shard_map/reduce_scatter | solution.py:243
  1336.8 62.3 %reduce-scatter.16.cloned.1.call-done = bf16[256,1536]{1,0:T(8,128)(2,1)} async-done(((bf16[2048,1536]{1,0:T(8,128)(2,1)}), bf16[256,1536]{1,0:T(8,128)(2,1)}) %reduce-scatter.16.cloned.1.call-update) | async-done | bytes 786448 | tf_op jit(solution)/shard_map/reduce_scatter | solution.py:217
  1402.0 131.5 %all-reduce.31.cloned.1.call-done = (f32[1536]{0:T(1024)}, f32[4,3072]{1,0:T(4,128)}, f32[3072]{0:T(1024)}, f32[4,256]{1,0:T(4,128)}, f32[256]{0:T(256)}, /*inde...) async-done(((f32[1536]{0:T(1024)}, f32[4,3072]{1,0:T(4,128)}, f32[3072]{0:T(1024)}, f32[4,256]{1,0:T(4,128)}, f32[256]{0:T(256)}, /*index=5*/f32[48]{0:T(128)}, ...) | async-done | bytes 85584 | tf_op jit(solution)/shard_map/psum | solution.py:299
  (1116 shorter events, 844.4 us)
Async XLA Ops:
  7.2 48.3 %all-gather.8.cloned.1.call-start = ((), (), s32[]{:S(2)}) async-start(), calls=%async_computation.8 | async-start | bytes 1474560 | tf_op jit(solution)/shard_map/all_gather | solution.py:162
  9.3 68.1 %all-gather.10.cloned.1.call-start = ((), (), s32[]{:S(2)}) async-start(), calls=%async_computation.9 | async-start | bytes 1474560 | tf_op jit(solution)/shard_map/all_gather | solution.py:163
  11.2 113.8 %all-gather.6.cloned.1.call-start = ((), (), s32[]{:S(2)}) async-start(), calls=%async_computation.7 | async-start | bytes 7077888 | tf_op jit(solution)/shard_map/all_gather | solution.py:171
  15.0 365.7 %all-gather.12.cloned.1.call-start = ((), (), s32[]{:S(2)}) async-start(), calls=%async_computation.10 | async-start | bytes 1474560 | tf_op jit(solution)/shard_map/all_gather | solution.py:166
  15.8 364.9 %all-gather.14.cloned.1.call-start = ((), (), s32[]{:S(2)}) async-start(), calls=%async_computation.12 | async-start | bytes 7077888 | tf_op jit(solution)/shard_map/all_gather | solution.py:224
  16.4 1131.3 %reduce-scatter.26.cloned.1.call-start = ((), (), s32[]{:S(2)}) async-start(), calls=%async_computation.17 | async-start | bytes 491520
  18.4 384.9 %copy-start.78 = (f32[384]{0:T(512)}, f32[384]{0:T(512)S(1)}, u32[]{:S(2)}) copy-start(f32[384]{0:T(512)S(1)} %dynamic_slice.119) | copy-start | bytes 4612
  19.3 383.9 %copy-start.46 = (f32[384]{0:T(512)}, f32[384]{0:T(512)S(1)}, u32[]{:S(2)}) copy-start(f32[384]{0:T(512)S(1)} %mul.729) | copy-start | bytes 4612
  1100.6 48.7 %reduce-scatter.20.cloned.1.call-start = ((), (), s32[]{:S(2)}) async-start(), calls=%async_computation.14 | async-start | bytes 983040 | tf_op jit(solution)/shard_map/reduce_scatter | solution.py:278
  1106.6 69.6 %reduce-scatter.28.cloned.1.call-start = ((), (), s32[]{:S(2)}) async-start(), calls=%async_computation.18 | async-start | bytes 1474560
  1115.7 90.9 %reduce-scatter.24.cloned.1.call-start = ((), (), s32[]{:S(2)}) async-start(), calls=%async_computation.16 | async-start | bytes 1474560
  1121.4 115.3 %reduce-scatter.22.cloned.1.call-start = ((), (), s32[]{:S(2)}) async-start(), calls=%async_computation.15 | async-start | bytes 1474560
  1123.8 209.9 %reduce-scatter.18.cloned.1.call-start = ((), (), s32[]{:S(2)}) async-start(), calls=%async_computation.13 | async-start | bytes 14155776 | tf_op jit(solution)/shard_map/reduce_scatter | solution.py:243
  1137.3 261.8 %reduce-scatter.16.cloned.1.call-start = ((), (), s32[]{:S(2)}) async-start(), calls=%async_computation.11 | async-start | bytes 7077888 | tf_op jit(solution)/shard_map/reduce_scatter | solution.py:217
  1144.9 188.9 %copy-start.14 = (bf16[256,1536]{1,0:T(8,128)(2,1)S(1)}, bf16[256,1536]{1,0:T(8,128)(2,1)}, u32[]{:S(2)}) copy-start(bf16[256,1536]{1,0:T(8,128)(2,1)} %param.22) | copy-start | bytes 2359300
  1144.9 188.8 %copy-start.36 = (f32[1536]{0:T(1024)S(1)}, f32[1536]{0:T(1024)}, u32[]{:S(2)}) copy-start(f32[1536]{0:T(1024)} %param.25) | copy-start | bytes 18436
  1145.0 388.6 %all-reduce.31.cloned.1.call-start = ((), (), s32[]{:S(2)}) async-start(), calls=%async_computation.19 | async-start | bytes 177152 | tf_op jit(solution)/shard_map/psum | solution.py:299
  1145.9 190.9 %copy-start.44 = (f32[3072]{0:T(1024)}, f32[3072]{0:T(1024)S(1)}, u32[]{:S(2)}) copy-start(f32[3072]{0:T(1024)S(1)} %dynamic_update_slice.73) | copy-start | bytes 36868
  1146.2 190.5 %copy-start.93 = (f32[48]{0:T(128)}, f32[48]{0:T(128)S(1)}, u32[]{:S(2)}) copy-start(f32[48]{0:T(128)S(1)} %dynamic_update_slice.72) | copy-start | bytes 580
  1146.5 190.3 %copy-start.94 = (f32[48]{0:T(128)}, f32[48]{0:T(128)S(1)}, u32[]{:S(2)}) copy-start(f32[48]{0:T(128)S(1)} %dynamic_update_slice.70) | copy-start | bytes 580
  1146.8 190.0 %copy-start.45 = (f32[3072]{0:T(1024)}, f32[3072]{0:T(1024)S(1)}, u32[]{:S(2)}) copy-start(f32[3072]{0:T(1024)S(1)} %dynamic_update_slice.69) | copy-start | bytes 36868
  1147.4 189.4 %copy-start.34 = (f32[4,3072]{1,0:T(4,128)}, f32[4,3072]{1,0:T(4,128)S(1)}, u32[]{:S(2)}) copy-start(f32[4,3072]{1,0:T(4,128)S(1)} %add_dynamic-update-slice_fusion) | copy-start | bytes 147460
  1147.6 189.1 %copy-start.92 = (f32[48]{0:T(128)}, f32[48]{0:T(128)S(1)}, u32[]{:S(2)}) copy-start(f32[48]{0:T(128)S(1)} %multiply_dynamic-update-slice_fusion) | copy-start | bytes 580
  1208.7 190.4 %copy-start.19 = (bf16[256,1536]{1,0:T(8,128)(2,1)S(1)}, bf16[256,1536]{1,0:T(8,128)(2,1)}, u32[]{:S(2)}) copy-start(bf16[256,1536]{1,0:T(8,128)(2,1)} %param.39) | copy-start | bytes 2359300
  (136 other events, 2699.9 us)
Sparse Core Ops, SparseCore 0:
  10.2 34.5 all-gather.7
  46.9 30.4 all-gather.9
  79.8 45.1 all-gather.5
  127.0 30.1 all-gather.11
  159.0 44.8 all-gather.13
  1100.7 18.8 reduce-scatter.25
  1122.6 22.7 reduce-scatter.19
  1147.8 28.3 reduce-scatter.27
  1178.6 27.8 reduce-scatter.23
  1208.8 27.8 reduce-scatter.21
  1240.6 93.0 reduce-scatter.17
  1337.4 61.7 reduce-scatter.15
  1406.7 126.7 all-reduce.30
where the time goes:
time: 1570 us; the launch traced here: 1550 us
  waiting for transfers between devices  440 us (28%)
  local copies, waits for them, and re-layouts  369 us (24%)
  other arithmetic  318 us (20%)
  matrix products  248 us (16%)
  blocking collectives  147 us (9%)
    dynamic_update_slice x32, local copies, waits for them, and re-layouts, ssd_scan(): _, outputs = lax.scan(jax.checkpoint(advance), zero_state, blocks)  164 us
    another operation x105, other arithmetic  140 us
    psum x1, waiting for transfers between devices, shards(): lax.psum((grad_norm_gain, conv_x_grad, conv_xb_grad, pulled[4], pulled[5]...  132 us
    reduce_scatter x1, waiting for transfers between devices, shards(): lax.psum_scatter(lax.dot_general(row_block, in_weight, contract_last, pre...  94.9 us
    psum x1, blocking collectives, shards(): grad_bc = lax.psum(pulled[1], ('row', 'col'))  88.3 us
    unnamed x17, waiting for transfers between devices  82.3 us
    dot_general x24, matrix products, advance(): inside = jnp.einsum('ijh,jhp->ihp', mixing, x_block, precision=HIGHEST)  68.2 us
    reduce_scatter x1, waiting for transfers between devices, shards(): lax.psum_scatter(jnp.dot(row_block, out_weight, preferred_element_type=jn...  62.3 us
  transfers between devices with their start and end apart: 13, of which 8 were waited for; matrix products, arithmetic and copies ran while one was open for 19% of the time, Pallas kernels for 0%

commit v1 on v0

v1 whole, which is shorter than its diff:
```python
import functools
import types

import jax
import jax.numpy as jnp
from jax import lax
from jax.experimental import pallas as pl
from jax.experimental.pallas import tpu as pltpu
from jax.sharding import PartitionSpec as P

SPAN = 256
HALF = SPAN // 2
STATE = 128
BC = 2 * STATE
KERNEL = 4
EPS = 1e-5
f32, bf16 = jnp.float32, jnp.bfloat16
MESH = pl.DeviceIdType.MESH


def nt(a, b):
    return lax.dot_general(a, b, (((1,), (1,)), ((), ())), preferred_element_type=f32)


def nn(a, b):
    return lax.dot_general(a, b, (((1,), (0,)), ((), ())), preferred_element_type=f32)


def tn(a, b):
    return lax.dot_general(a, b, (((0,), (0,)), ((), ())), preferred_element_type=f32)


def aligned(start, size):
    return pl.ds(pl.multiple_of(start, size), size)


def softplus(v):
    return jnp.maximum(v, 0.0) + jnp.log1p(jnp.exp(-jnp.abs(v)))


def split3(v):
    a = v.astype(bf16)
    w = v - a.astype(f32)
    b = w.astype(bf16)
    return jnp.concatenate([a, b, (w - b.astype(f32)).astype(bf16)], axis=0)


def merge3(v):
    return v[0:8] + v[8:16] + v[16:24]


def tri_low():
    i = lax.broadcasted_iota(jnp.int32, (SPAN, SPAN), 0)
    j = lax.broadcasted_iota(jnp.int32, (SPAN, SPAN), 1)
    return (i >= j).astype(bf16)


def decay_terms(b, offs, da):
    first = b * SPAN
    row = first + lax.broadcasted_iota(jnp.int32, (1, SPAN), 1)
    col = first + lax.broadcasted_iota(jnp.int32, (SPAN, 1), 0)

    def begin(pos):
        at = jnp.zeros_like(pos)
        for o in offs[1:]:
            at = jnp.where(pos >= o, o, at)
        return at

    beg_r, beg_c = begin(row), begin(col)
    l_row = merge3(nt(split3(da), tri_low()))
    l_col = l_row.T
    last = l_row[:, SPAN - 1 : SPAN]
    end_b = jnp.max(beg_r, axis=1, keepdims=True)
    e = jnp.where(beg_r < first, jnp.exp(l_row), 0.0)
    we = jnp.where(beg_r == end_b, jnp.exp(last - l_row), 0.0)
    kept = jnp.where(end_b < first, jnp.exp(last), 0.0)
    mask = jnp.where((beg_r == beg_c) & (row <= col), 1.0, 0.0)
    return l_row, l_col, e, we, kept, mask, row - beg_r


def wide(ref, k, rows):
    w = ref[k, rows, :]
    return jnp.concatenate([w, w], axis=1)


def fold(v):
    return v[:, 0:128] + v[:, 128:256]


def conv_forward(cur, tail, pref, rows, places):
    win = jnp.concatenate([tail, cur], axis=1)
    u = wide(pref, 3, rows) * cur + wide(pref, 4, rows)
    for s in (1, 2, 3):
        back = jnp.where(places >= s, pltpu.roll(win, s, 1)[:, 128:], 0.0)
        u = u + wide(pref, 3 - s, rows) * back
    return u


def conv_backward(R, raw, du, pref, acc, head, rows, base, tok, m):
    out = wide(pref, 3, rows) * du
    acc[4, rows, :] += fold(du)
    acc[3, rows, :] += fold(du * raw)
    for s in (1, 2, 3):
        w = du * m[s]
        win = jnp.concatenate([w, head[s - 1, rows, :]], axis=1)
        sh = pltpu.roll(win, SPAN + 128 - s, 1)[:, 0:SPAN]
        head[s - 1, rows, :] = w[:, 0:128]
        out = out + wide(pref, 3 - s, rows) * sh
        acc[3 - s, rows, :] += fold(sh * raw)
    R.dcat[base + rows.start : base + rows.stop, tok] = out.astype(bf16)


def fwd_block(b, R, offs, C, H):
    p = C // H
    tok = aligned(b * SPAN, SPAN)
    R.pr[...] = nt(R.wcat[...], R.hn[tok, :])
    R.z[:, tok] = R.pr[0:C, :].astype(bf16)
    R.xr[:, tok] = R.pr[C : 2 * C, :].astype(bf16)
    R.bcr[:, tok] = R.pr[2 * C : 2 * C + BC, :].astype(bf16)
    dr = R.pr[2 * C + BC : 2 * C + BC + 8, :] + R.ph[:, 0:1]
    R.dr[:, tok] = dr
    dt = softplus(dr)
    l_row, l_col, e, we, kept, mask, places = decay_terms(b, offs, dt * R.ph[:, 1:2])
    bcr = R.pr[2 * C : 2 * C + BC, :]
    u = conv_forward(bcr, R.tail_bc[...], R.pbc, slice(0, BC), places).astype(bf16)
    R.tail_bc[...] = bcr[:, 128:]
    R.ubc[:, tok] = u
    u = u.astype(f32)
    bc = (u * jax.nn.sigmoid(u)).astype(bf16)
    bt, ct = bc[0:STATE, :], bc[STATE:BC, :]
    R.gm[...] = tn(ct, bt) * mask
    sq = jnp.zeros((1, SPAN), f32)
    for h in range(H):
        rows = slice(h * p, (h + 1) * p)
        hh = slice(h, h + 1)
        xr = R.pr[C + h * p : C + (h + 1) * p, :]
        u = conv_forward(xr, R.tail_x[rows, :], R.px, rows, places).astype(bf16)
        R.tail_x[rows, :] = xr[:, 128:]
        R.ux[rows, tok] = u
        u = u.astype(f32)
        x = u * jax.nn.sigmoid(u)
        xd = x * dt[hh, :]
        d = jnp.exp(jnp.minimum(l_col[:, hh] - l_row[hh, :], 0.0))
        mix = (d * R.gm[...]).astype(bf16)
        st = R.state[rows, :]
        stb = st.astype(bf16)
        R.states[b, rows, :] = stb
        y = nt(xd.astype(bf16), mix) + nn(stb, ct) * e[hh, :]
        R.y[rows, tok] = y
        R.state[rows, :] = kept[hh, :] * st + nt((xd * we[hh, :]).astype(bf16), bt)
        zz = R.z[rows, tok].astype(f32)
        gy = (y + wide(R.px, 6, rows) * x) * (zz * jax.nn.sigmoid(zz))
        sq = sq + jnp.sum(gy * gy, axis=0, keepdims=True)
        R.gg[rows, tok] = (gy * wide(R.px, 5, rows)).astype(bf16)
    R.sums[pl.ds(b, 1), :] = sq


def bwd_block(b, R, offs, C, H, inner):
    p = C // H
    nb = R.sums.shape[0] // 2
    tok = aligned(b * SPAN, SPAN)
    v = R.dr[:, tok]
    dt = softplus(v)
    rate = R.ph[:, 1:2]
    l_row, l_col, e, we, kept, mask, places = decay_terms(b, offs, dt * rate)
    ubc = R.ubc[:, tok].astype(f32)
    sg = jax.nn.sigmoid(ubc)
    bc = (ubc * sg).astype(bf16)
    bt, ct = bc[0:STATE, :], bc[STATE:BC, :]
    R.gm[...] = tn(ct, bt) * mask
    r = lax.rsqrt(R.tot[pl.ds(b, 1), :] / inner + EPS)
    rs = r * r * r * R.tot[pl.ds(nb + b, 1), :] / inner
    m = [None] + [jnp.where(places >= s, 1.0, 0.0) for s in (1, 2, 3)]
    decays, directs, ends = [], [], []
    for h in range(H):
        rows = slice(h * p, (h + 1) * p)
        hh = slice(h, h + 1)
        u = R.ux[rows, tok].astype(f32)
        sx = jax.nn.sigmoid(u)
        x = u * sx
        y = R.y[rows, tok]
        zz = R.z[rows, tok].astype(f32)
        sz = jax.nn.sigmoid(zz)
        gate = zz * sz
        skip = wide(R.px, 6, rows)
        yf = y + skip * x
        gy = yf * gate
        dyn = R.dyn[rows, tok].astype(f32)
        gyr = gy * r
        R.accx[5, rows, :] += fold(dyn * gyr)
        dgy = (r * wide(R.px, 5, rows)) * dyn - gy * rs
        R.dcat[rows, tok] = (dgy * yf * (sz + gate * (1.0 - sz))).astype(bf16)
        dy = dgy * gate
        dyb = dy.astype(bf16)
        R.accx[6, rows, :] += fold(dy * x)
        xd = x * dt[hh, :]
        xdb = xd.astype(bf16)
        d = jnp.exp(jnp.minimum(l_col[:, hh] - l_row[hh, :], 0.0))
        mix = (d * R.gm[...]).astype(bf16)
        vin = nn(dyb, mix)
        dm = tn(dyb, xdb) * d
        if h == 0:
            R.dg[...] = dm
        else:
            R.dg[...] += dm
        stb = R.states[b, rows, :]
        lam = R.state[rows, :]
        lamb = lam.astype(bf16)
        lb = nn(lamb, bt) * we[hh, :]
        vt = vin + lb
        xlow = xdb.astype(f32)
        decays.append(jnp.sum(dyb.astype(f32) * y - xlow * vt, axis=0, keepdims=True))
        directs.append(jnp.sum(x * vt, axis=0, keepdims=True))
        through = jnp.sum(lam * stb.astype(f32), axis=0, keepdims=True) * kept[hh, :]
        ends.append(
            jnp.sum(xlow * lb, axis=0, keepdims=True)
            + jnp.concatenate([through, jnp.zeros((1, SPAN - STATE), f32)], axis=1)
        )
        edy = (dy * e[hh, :]).astype(bf16)
        R.edy[rows, :] = edy
        R.wxd[rows, :] = (xd * we[hh, :]).astype(bf16)
        R.lamb[rows, :] = lamb
        R.state[rows, :] = kept[hh, :] * lam + nt(edy, ct)
        dx = dt[hh, :] * vt + skip * dy
        du = dx * (sx + x * (1.0 - sx))
        conv_backward(R, R.xr[rows, tok].astype(f32), du, R.px, R.accx, R.head_x, rows, C, tok, m)
    dgm = (R.dg[...] * mask).astype(bf16)
    dct = nt(bt, dgm) + tn(R.states[b], R.edy[...])
    dbt = nn(ct, dgm) + tn(R.lamb[...], R.wxd[...])
    du = jnp.concatenate([dbt, dct], axis=0) * (sg + ubc * sg * (1.0 - sg))
    conv_backward(
        R, R.bcr[:, tok].astype(f32), du, R.pbc, R.accbc, R.head_bc, slice(0, BC), 2 * C, tok, m
    )
    pad = [jnp.zeros((8 - H, SPAN), f32)]
    end = jnp.sum(jnp.concatenate(ends + pad, axis=0), axis=1, keepdims=True)
    g = merge3(nn(split3(jnp.concatenate(decays + pad, axis=0)), tri_low())) + end
    ddr = (g * rate + jnp.concatenate(directs + pad, axis=0)) * jax.nn.sigmoid(v)
    R.acch[0] += ddr
    R.acch[1] += g * dt * rate
    R.dcat[2 * C + BC : 2 * C + BC + 16, tok] = jnp.concatenate(
        [ddr, jnp.zeros((8, SPAN), f32)], axis=0
    ).astype(bf16)


def remote(src, dst, send, recv, device):
    return pltpu.make_async_remote_copy(
        src_ref=src, dst_ref=dst, send_sem=send, recv_sem=recv, device_id=device, device_id_type=MESH
    )


class Place:
    def __init__(self, n):
        self.n = n
        self.dp, self.row, self.col = (lax.axis_index(a) for a in ("dp", "row", "col"))
        self.x, self.c, self.y = self.row // 2, self.row % 2, self.col
        self.q = self.index(self.x, self.c, self.y)
        self.mate = (self.dp, self.x * 2 + 1 - self.c, self.y)
        self.xn = (self.dp, (1 - self.x) * 2 + self.c, self.y)
        self.yn = (self.dp, self.row, 1 - self.y)
        self.diag = (self.dp, (1 - self.x) * 2 + self.c, 1 - self.y)

    def index(self, x, c, y):
        return (x * 2 + c) * 2 + y

    def plane(self, d):
        k = (self.q + d) % 8
        return k, (self.dp, k // 2, k % 2)

    def line(self, d):
        k = (self.dp + d) % self.n
        return k, (k, self.row, self.col)

    def right(self):
        return (self.dp + 1, self.row, self.col)

    def left(self):
        return (self.dp - 1, self.row, self.col)


class PlaneGather:
    def __init__(self, me, buf, send, recv):
        self.me, self.buf, self.send, self.recv = me, buf, send, recv
        x, c, y = me.x, me.c, me.y
        own = lambda cc: (
            me.index(x, cc, y),
            me.index(1 - x, cc, y),
            me.index(x, cc, 1 - y),
            me.index(1 - x, cc, 1 - y),
        )
        self.q, self.qx, self.qy, self.qd = own(c)
        self.mq, self.mx, self.my, self.md = own(1 - c)

    def at(self, k, half):
        if half is None:
            return self.buf.at[aligned(k * SPAN, SPAN), :]
        return self.buf.at[aligned(k * SPAN + half * HALF, HALF), :]

    def copy(self, i, k, half, device):
        region = self.at(k, half)
        return remote(region, region, self.send.at[i], self.recv.at[i], device)

    def wait(self, i, k, half):
        self.copy(i, k, half, self.me.mate).wait_recv()

    def start(self):
        me = self.me
        self.copy(0, self.q, 0, me.xn).start()
        self.copy(3, self.q, 1, me.yn).start()
        self.copy(1, self.q, 1, me.xn).start()
        self.copy(2, self.q, 0, me.yn).start()
        self.copy(6, self.q, None, me.mate).start()

    def step1(self):
        me = self.me
        self.wait(0, self.qx, 0)
        self.copy(4, self.qx, 0, me.yn).start()
        self.copy(7, self.qx, 0, me.mate).start()
        self.wait(3, self.qy, 1)
        self.copy(5, self.qy, 1, me.xn).start()
        self.copy(10, self.qy, 1, me.mate).start()

    def step2(self):
        me = self.me
        self.wait(1, self.qx, 1)
        self.copy(8, self.qx, 1, me.mate).start()
        self.wait(2, self.qy, 0)
        self.copy(9, self.qy, 0, me.mate).start()

    def step3(self):
        me = self.me
        self.wait(4, self.qd, 0)
        self.copy(11, self.qd, 0, me.mate).start()
        self.wait(5, self.qd, 1)
        self.copy(12, self.qd, 1, me.mate).start()

    def step4(self):
        self.wait(6, self.mq, None)
        self.wait(7, self.mx, 0)
        self.wait(8, self.mx, 1)
        self.wait(9, self.my, 0)
        self.wait(10, self.my, 1)
        self.wait(11, self.md, 0)
        self.wait(12, self.md, 1)
        for i in range(13):
            self.copy(i, self.q, None if i == 6 else 0, self.me.mate).wait_send()


def both(*conds):
    out = conds[0]
    for c in conds[1:]:
        out = jnp.logical_and(out, c)
    return out


class LineGather:
    def __init__(self, me, at, send, recv):
        self.me, self.at, self.send, self.recv = me, at, send, recv

    def copy(self, way, s, k):
        device = self.me.right() if way == 0 else self.me.left()
        return remote(self.at(k), self.at(k), self.send.at[way, s], self.recv.at[way, s], device)

    def start(self):
        me = self.me

        @pl.when(me.dp < me.n - 1)
        def _():
            self.copy(0, 0, me.dp).start()

        @pl.when(me.dp > 0)
        def _():
            self.copy(1, 0, me.dp).start()

    def step(self, s):
        me = self.me
        k = me.dp - 1 - s

        @pl.when(k >= 0)
        def _():
            self.copy(0, s, k).wait_recv()

            @pl.when(both(me.dp < me.n - 1, s < me.n - 2))
            def _():
                self.copy(0, s + 1, k).start()

        j = me.dp + 1 + s

        @pl.when(j <= me.n - 1)
        def _():
            self.copy(1, s, j).wait_recv()

            @pl.when(both(me.dp > 0, s < me.n - 2))
            def _():
                self.copy(1, s + 1, j).start()

    def finish(self, s):
        me = self.me

        @pl.when(both(me.dp < me.n - 1, me.dp - s >= 0))
        def _():
            self.copy(0, s, me.dp).wait_send()

        @pl.when(both(me.dp > 0, me.dp + s <= me.n - 1))
        def _():
            self.copy(1, s, me.dp).wait_send()


class LineScatter:
    def __init__(self, me, src, slot, send, recv):
        self.me, self.src, self.slot, self.send, self.recv = me, src, slot, send, recv

    def copy(self, way, s, what, to):
        (a, i), (b, j) = what, to
        device = self.me.right() if way == 0 else self.me.left()
        return remote(a.at[i], b.at[j], self.send.at[way, s], self.recv.at[way, s], device)

    def got(self, way, s, slot):
        self.copy(way, s, slot, slot).wait_recv()

    def add(self, k):
        (a, i), (b, j) = self.slot(k), self.src(k)
        a[i] = (a[i].astype(f32) + b[j].astype(f32)).astype(bf16)

    def step(self, s):
        me, n = self.me, self.me.n
        k = n - 1 - s

        @pl.when(k > me.dp)
        def _():
            @pl.when(me.dp > 0)
            def _():
                self.got(0, s, self.slot(k))
                self.add(k)
                self.copy(0, s, self.slot(k), self.slot(k)).start()

            @pl.when(me.dp == 0)
            def _():
                self.copy(0, s, self.src(k), self.slot(k)).start()

        j = s

        @pl.when(j < me.dp)
        def _():
            to = self.slot(jnp.where(j == me.dp - 1, n, j))

            @pl.when(me.dp < n - 1)
            def _():
                self.got(1, s, self.slot(j))
                self.add(j)
                self.copy(1, s, self.slot(j), to).start()

            @pl.when(me.dp == n - 1)
            def _():
                self.copy(1, s, self.src(j), to).start()

    def total(self, put):
        me, n = self.me, self.me.n
        a, i = self.src(me.dp)
        put(a[i].astype(f32), True)

        @pl.when(me.dp > 0)
        def _():
            b, j = self.slot(me.dp)
            self.got(0, n - 1 - me.dp, (b, j))
            put(b[j].astype(f32), False)

        @pl.when(me.dp < n - 1)
        def _():
            b, j = self.slot(n)
            self.got(1, me.dp, (b, j))
            put(b[j].astype(f32), False)

    def finish(self, s):
        me, n = self.me, self.me.n

        @pl.when(s < n - 1 - me.dp)
        def _():
            self.copy(0, s, self.src(0), self.slot(0)).wait_send()

        @pl.when(s < me.dp)
        def _():
            self.copy(1, s, self.src(0), self.slot(0)).wait_send()


class PlaneScatter:
    def __init__(self, me, R, send, recv, part, credit):
        self.me, self.R, self.send, self.recv, self.part, self.credit = me, R, send, recv, part, credit
        x, y = me.x, me.y
        self.jo, self.jx, self.jy, self.jd = x * 2 + y, (1 - x) * 2 + y, x * 2 + 1 - y, (1 - x) * 2 + 1 - y

    def copy(self, i, src, dst, device):
        return remote(src, dst, self.send.at[i], self.recv.at[i], device)

    def first(self):
        me, R = self.me, self.R
        if self.credit:
            pl.semaphore_wait(R.free.at[0], 1)

        @pl.loop(0, 4)
        def _(j):
            k = me.index(j // 2, 1 - me.c, j % 2)

            @pl.when(j >= 2)
            def _():
                self.copy(j - 2, R.sb.at[j % 2], R.rb.at[j - 2], me.mate).wait_send()

            R.sb[j % 2, 0] = self.part(k, 0).astype(bf16)
            R.sb[j % 2, 1] = self.part(k, 1).astype(bf16)
            self.copy(j, R.sb.at[j % 2], R.rb.at[j], me.mate).start()

    def second(self):
        me, R = self.me, self.R
        if self.credit:
            pl.semaphore_wait(R.free.at[1], 1)
            pl.semaphore_wait(R.free.at[2], 1)

        @pl.loop(0, 4)
        def _(t):
            dx, dy = 1 - t // 2, 1 - t % 2
            xx = me.x + dx * (1 - 2 * me.x)
            yy = me.y + dy * (1 - 2 * me.y)
            j = xx * 2 + yy
            k = me.index(xx, me.c, yy)
            self.copy(j, R.sb.at[0], R.rb.at[j], me.mate).wait_recv()
            R.rb[j, 0] = (self.part(k, 0) + R.rb[j, 0].astype(f32)).astype(bf16)
            R.rb[j, 1] = (self.part(k, 1) + R.rb[j, 1].astype(f32)).astype(bf16)

            @pl.when(t == 0)
            def _():
                self.copy(4, R.rb.at[self.jd, 0], R.da, me.xn).start()
                self.copy(5, R.rb.at[self.jd, 1], R.db, me.yn).start()

            @pl.when(t == 1)
            def _():
                self.copy(6, R.rb.at[self.jx, 0], R.fx.at[0], me.xn).start()

            @pl.when(t == 2)
            def _():
                self.copy(9, R.rb.at[self.jy, 1], R.fy.at[1], me.yn).start()

    def relay(self):
        me, R = self.me, self.R
        self.copy(4, R.da, R.da, me.xn).wait_recv()
        R.rb[self.jy, 0] = (R.rb[self.jy, 0].astype(f32) + R.da[...].astype(f32)).astype(bf16)
        self.copy(8, R.rb.at[self.jy, 0], R.fy.at[0], me.yn).start()
        self.copy(5, R.db, R.db, me.yn).wait_recv()
        R.rb[self.jx, 1] = (R.rb[self.jx, 1].astype(f32) + R.db[...].astype(f32)).astype(bf16)
        self.copy(7, R.rb.at[self.jx, 1], R.fx.at[1], me.xn).start()

    def total(self, put):
        me, R = self.me, self.R
        for half in (0, 1):
            self.copy(6 + half, R.fx.at[half], R.fx.at[half], me.xn).wait_recv()
            self.copy(8 + half, R.fy.at[half], R.fy.at[half], me.yn).wait_recv()
            steps = R.da.shape[0] // 128

            @pl.loop(0, steps)
            def _(i):
                rows = aligned(i * 128, 128)
                v = R.rb[self.jo, half, rows, :].astype(f32)
                put(half * steps + i, v + R.fx[half, rows, :].astype(f32) + R.fy[half, rows, :].astype(f32))

    def finish(self, release):
        me, R = self.me, self.R
        for i in (2, 3):
            self.copy(i, R.sb.at[i % 2], R.rb.at[i], me.mate).wait_send()
        for i in range(4, 10):
            self.copy(i, R.da, R.db, me.mate).wait_send()
        if release:
            for i, device in enumerate((me.mate, me.xn, me.yn)):
                pl.semaphore_signal(R.free.at[i], 1, device_id=device, device_id_type=MESH)


def stepped(n, *fns):
    if n <= 4:
        return [lambda s=s: [f(s) for f in fns] for s in range(n - 1)]

    def every():
        @pl.loop(0, n - 1)
        def _(s):
            for f in fns:
                f(s)

    return [every] + [lambda: None] * 2


def kernel(names, n, C, H, inner, *refs):
    R = types.SimpleNamespace(**dict(zip(names, refs)))
    me = Place(n)
    T, D = R.hn.shape
    nb = T // SPAN
    DS = D // n
    dp = me.dp
    dt_rows = slice(2 * C + BC, 2 * C + BC + 16)
    mine = aligned(me.q * SPAN, SPAN)
    share = lambda k: pl.ds(pl.multiple_of(k * DS, 16), DS)
    dhalf = lambda h: slice(h * (D // 2), (h + 1) * (D // 2))
    half = aligned(2 * C + me.c * 128, 128)
    other = aligned(2 * C + (1 - me.c) * 128, 128)

    barrier = pltpu.get_barrier_semaphore()
    for d in range(1, 8):
        pl.semaphore_signal(barrier, 1, device_id=me.plane(d)[1], device_id_type=MESH)
    for d in range(1, n):
        pl.semaphore_signal(barrier, 1, device_id=me.line(d)[1], device_id_type=MESH)

    stage = lambda a, z: R.y.at[0:DS, a:z]
    arriving = [
        pltpu.make_async_copy(src, dst, R.loc.at[i])
        for i, (src, dst) in enumerate(
            (
                (R.wx, stage(C, 2 * C)),
                (R.wbc, stage(2 * C, 2 * C + BC)),
                (R.wz, stage(0, C)),
                (R.gcot, R.cot.at[mine, :]),
            )
        )
    ]
    for copy in arriving:
        copy.start()
    @pl.loop(0, SPAN // 32)
    def _(i):
        u = R.hid[aligned(i * 32, 32), :].astype(f32)
        qn = lax.rsqrt(jnp.mean(u * u, axis=1, keepdims=True) + EPS)
        R.hn[aligned(me.q * SPAN + i * 32, 32), :] = (u * qn * R.gain[...]).astype(bf16)

    for copy in arriving:
        copy.wait()
    R.wd[share(dp), 0 : 2 * C] = R.y[0:DS, 0 : 2 * C].astype(bf16)
    R.wd[share(dp), half] = R.y[0:DS, half].astype(bf16)
    R.wot[share(dp), :] = R.wo[...].T.astype(bf16)
    R.wdt[dp] = R.wdt_own[...]
    pl.semaphore_wait(barrier, 7 + n - 1)

    tokens = PlaneGather(me, R.hn, R.ag_s.at[0], R.ag_r.at[0])
    cots = PlaneGather(me, R.cot, R.ag_s.at[1], R.ag_r.at[1])
    places = (
        lambda k: R.wd.at[share(k), C : 2 * C],
        lambda k: R.wd.at[share(k), half],
        lambda k: R.wdt.at[k],
        lambda k: R.wd.at[share(k), 0:C],
        lambda k: R.wot.at[share(k), :],
    )
    gathers = [LineGather(me, at, R.za_s.at[i], R.za_r.at[i]) for i, at in enumerate(places)]
    first, wo_gather = gathers[:4], gathers[4]
    tokens.start()
    for g in first:
        g.start()

    for k in range(7):
        R.px[k] = jnp.broadcast_to(R.pxc[:, k : k + 1], (C, 128))
    for k in range(5):
        R.pbc[k] = jnp.broadcast_to(R.pbcc[:, k : k + 1], (BC, 128))
    for a in (R.tail_bc, R.tail_x, R.state, R.head_x, R.head_bc, R.accx, R.accbc, R.acch, R.sv):
        a[...] = jnp.zeros_like(a)
    offs = [R.offs[k] for k in range(R.offs.shape[0])]

    line = stepped(n, *[g.step for g in first])
    tokens.step1()
    line[0]()
    tokens.step2()
    line[1]()
    tokens.step3()
    cots.start()
    line[2]()
    bc_swap = remote(R.wd.at[:, half], R.wd.at[:, half], R.mate_s.at[0], R.mate_r.at[0], me.mate)
    bc_swap.start()
    wo_gather.start()
    tokens.step4()
    remote(R.wd.at[:, other], R.wd.at[:, other], R.mate_s.at[0], R.mate_r.at[0], me.mate).wait_recv()
    bc_swap.wait_send()
    for s in stepped(n, *[g.finish for g in first]):
        s()
    for k in range(0, 2 * C + BC, 256):
        R.wcat[k : k + 256, :] = R.wd[:, k : k + 256].T
    for k in range(n):
        R.wcat[dt_rows, k * DS : (k + 1) * DS] = R.wdt[k]
    pad = jnp.zeros((112, D), bf16)
    R.wd[:, 2 * C + BC : 2 * C + BC + 128] = jnp.concatenate([R.wcat[dt_rows, :], pad], axis=0).T

    line = stepped(n, wo_gather.step)
    beside = {3: [cots.step1, line[0]], 5: [line[1]], 6: [cots.step2], 7: [line[2]]}

    @pl.loop(0, nb)
    def _(b):
        fwd_block(b, R, offs, C, H)
        for k, fns in beside.items():

            @pl.when(b == min(k, nb - 1))
            def _():
                for f in fns:
                    f()

    cots.step3()
    cots.step4()
    for s in stepped(n, wo_gather.finish):
        s()
    for k in range(0, D, 256):
        R.wout[:, k : k + 256] = R.wot[k : k + 256, :].T

    @pl.loop(0, nb)
    def _(b):
        tok = aligned(b * SPAN, SPAN)
        dyn = nt(R.wout[...], R.cot[tok, :])
        R.dyn[:, tok] = dyn.astype(bf16)
        R.sums[pl.ds(nb + b, 1), :] = jnp.sum(dyn * R.gg[:, tok].astype(f32), axis=0, keepdims=True)

    for d in range(1, 8):
        k, device = me.plane(d)
        remote(R.sums, R.sslot.at[me.q], R.sum_s.at[k], R.sum_r.at[me.q], device).start()
    R.sslot[me.q] = R.sums[...]

    mixed = PlaneScatter(
        me, R, R.rs_s.at[0], R.rs_r.at[0], lambda k, h: nn(R.wot[dhalf(h), :], R.gg[:, aligned(k * SPAN, SPAN)]), False
    )
    mixed.first()
    mixed.second()
    for d in range(1, 8):
        k, device = me.plane(d)
        remote(R.sums, R.sslot.at[k], R.sum_s.at[k], R.sum_r.at[k], device).wait()
    total = R.sslot[0]
    for k in range(1, 8):
        total = total + R.sslot[k]
    R.tot[...] = total

    @pl.loop(0, nb)
    def _(b):
        tok = aligned(b * SPAN, SPAN)
        r = lax.rsqrt(R.tot[pl.ds(b, 1), :] / inner + EPS)
        R.gg[:, tok] = (R.gg[:, tok].astype(f32) * r).astype(bf16)

    @pl.loop(0, D // 256)
    def _(i):
        some = aligned(i * 256, 256)
        R.wot[some, :] = nn(R.gg[...], R.cot[:, some]).astype(bf16).T

    @pl.when(dp < n - 1)
    def _():
        pl.semaphore_signal(R.free.at[3], 1, device_id=me.right(), device_id_type=MESH)

    @pl.when(dp > 0)
    def _():
        pl.semaphore_signal(R.free.at[4], 1, device_id=me.left(), device_id_type=MESH)

    @pl.when(dp > 0)
    def _():
        pl.semaphore_wait(R.free.at[3], 1)

    @pl.when(dp < n - 1)
    def _():
        pl.semaphore_wait(R.free.at[4], 1)

    def scatter(i, src, lanes):
        slot = lambda k: (R.cot, (share(k), slice(*lanes)))
        return LineScatter(me, src, slot, R.zr_s.at[i], R.zr_r.at[i])

    wo_sum = scatter(0, lambda k: (R.wot, (share(k), slice(0, C))), (2 * C + 128, 3 * C + 128))
    x_sum = scatter(1, lambda k: (R.wd, (share(k), slice(C, 2 * C))), (C, 2 * C))
    z_sum = scatter(2, lambda k: (R.wd, (share(k), slice(0, C))), (0, C))
    bc_sum = scatter(3, lambda k: (R.wd, (share(k), half)), (2 * C, 2 * C + 128))
    dt_sum = LineScatter(
        me, lambda k: (R.gdt, (k,)), lambda k: (R.rdt, (k,)), R.zr_s.at[4], R.zr_r.at[4]
    )

    def put(ref):
        def f(v, new):
            if new:
                ref[...] = v
            else:
                ref[...] += v

        return f

    out_copy = pltpu.make_async_copy(R.wout.at[0:SPAN, :], R.block_out, R.loc.at[5])

    def finish_mixed():
        r = lax.rsqrt(R.tot[pl.ds(me.q, 1), :] / inner + EPS)

        def put(k, v):
            cols = aligned(k * 128, 128)
            R.wout[0:SPAN, cols] = (R.hid[:, cols].astype(f32) + (v * r).T).astype(bf16)

        mixed.total(put)
        out_copy.start()
        mixed.finish(True)

    R.state[...] = jnp.zeros_like(R.state)
    line = stepped(n, wo_sum.step)
    beside = {1: [mixed.relay, line[0]], 3: [line[1]], 5: [line[2]], 6: [finish_mixed]}

    @pl.loop(0, nb)
    def _(i):
        bwd_block(nb - 1 - i, R, offs, C, H, inner)
        for k, fns in beside.items():

            @pl.when(i == min(k, nb - 1))
            def _():
                for f in fns:
                    f()

    rows = 2 * C + BC + 16
    dhn = PlaneScatter(
        me,
        R,
        R.rs_s.at[1],
        R.rs_r.at[1],
        lambda k, h: nn(R.wd[dhalf(h), 0:rows], R.dcat[:, aligned(k * SPAN, SPAN)]),
        True,
    )
    dhn.first()
    dhn.second()

    def weight_grad(a, z):
        @pl.loop(0, D // 256)
        def _(i):
            some = aligned(i * 256, 256)
            g = nn(R.dcat[a:z, :], R.hn[:, some])
            R.ng[:, some] += jnp.sum(g * R.wcat[a:z, some].astype(f32), axis=0, keepdims=True)
            g = g.astype(bf16)
            R.wd[some, a : a + 256] = g[0:256].T
            if z - a > 256:
                R.gdt_all[:, some] = g[256:272]

    R.ng[...] = jnp.zeros_like(R.ng)
    weight_grad(2 * C, rows)
    for k in range(n):
        R.gdt[k] = R.gdt_all[:, k * DS : (k + 1) * DS]
    bx = R.cot.at[0:D, 3 * C + 128 : 3 * C + 256]
    bc_pair = remote(R.wd.at[:, other], bx, R.mate_s.at[1], R.mate_r.at[1], me.mate)
    bc_pair.start()
    for a in (2 * C - 256, 2 * C - 512):
        weight_grad(a, a + 256)
    bc_pair.wait()
    R.wd[:, half] = (R.wd[:, half].astype(f32) + bx[...].astype(f32)).astype(bf16)
    line = stepped(n, x_sum.step, bc_sum.step, dt_sum.step)
    line[0]()
    dhn.relay()
    for a in range(2 * C - 768, -1, -256):
        weight_grad(a, a + 256)
    zline = stepped(n, z_sum.step)
    zline[0]()

    ax = [jnp.sum(R.accx[k], axis=1, keepdims=True) for k in range(7)]
    ab = [jnp.sum(R.accbc[k], axis=1, keepdims=True) for k in range(5)]
    R.sv[0:8, :] = jnp.concatenate(ax + [jnp.zeros((C, 1), f32)], axis=1).T
    R.sv[8:16, 0:BC] = jnp.concatenate(ab + [jnp.zeros((BC, 3), f32)], axis=1).T
    ng = R.ng[...] / R.gain[...]
    for k in range(D // C):
        R.sv[16 + k : 17 + k, :] = ng[:, k * C : (k + 1) * C]
    for k in range(2):
        R.sv[24 + 8 * k : 32 + 8 * k, 0:128] = jnp.broadcast_to(
            jnp.sum(R.acch[k], axis=1, keepdims=True), (8, 128)
        )
    for d in range(1, n):
        k, device = me.line(d)
        remote(R.sv, R.lslot.at[dp], R.ls_s.at[k], R.ls_r.at[dp], device).start()
    R.lslot[dp] = R.sv[...]
    line[1]()
    zline[1]()
    for d in range(1, n):
        k, device = me.line(d)
        remote(R.sv, R.lslot.at[k], R.ls_s.at[k], R.ls_r.at[k], device).wait()
    total = R.lslot[0]
    for k in range(1, n):
        total = total + R.lslot[k]
    R.pv[...] = total
    for d in range(1, 8):
        k, device = me.plane(d)
        remote(R.pv, R.small.at[me.q], R.ps_s.at[k], R.ps_r.at[me.q], device).start()
    R.small[me.q] = total
    line[2]()
    zline[2]()

    x_sum.total(put(R.gx))
    bc_sum.total(put(R.bsum))
    j = me.x * 2 + me.y
    R.bslot[j] = R.bsum[...].astype(bf16)
    crossing = []
    for i, (device, k) in enumerate(
        ((me.xn, (1 - me.x) * 2 + me.y), (me.yn, me.x * 2 + 1 - me.y), (me.diag, (1 - me.x) * 2 + 1 - me.y))
    ):
        remote(R.bslot.at[j], R.bslot.at[j], R.bc_s.at[i], R.bc_r.at[i], device).start()
        crossing.append(remote(R.bslot.at[k], R.bslot.at[k], R.bc_s.at[i], R.bc_r.at[i], device))
    z_sum.total(put(R.gz))
    dt_sum.total(put(R.gdt_out))
    wo_sum.total(put(R.gwo))
    for c in crossing:
        c.wait()
    v = R.bslot[0].astype(f32)
    for k in range(1, 4):
        v = v + R.bslot[k].astype(f32)
    R.bfin[me.c] = v.astype(bf16)
    bc_last = remote(R.bfin.at[me.c], R.bfin.at[me.c], R.mate_s.at[2], R.mate_r.at[2], me.mate)
    bc_last.start()

    cot_again = pltpu.make_async_copy(R.gcot, R.hn.at[0:SPAN, :], R.loc.at[4])
    cot_again.start()
    def put_dh(k, v):
        R.y[0:SPAN, aligned(k * 128, 128)] = v.T

    dhn.total(put_dh)
    cot_again.wait()

    @pl.loop(0, SPAN // 32)
    def _(i):
        some = aligned(i * 32, 32)
        u = R.hid[some, :].astype(f32)
        qn = lax.rsqrt(jnp.mean(u * u, axis=1, keepdims=True) + EPS)
        w = R.y[some, 0:D] * R.gain[...]
        dot = jnp.sum(w * u, axis=1, keepdims=True) / D
        R.hn[aligned(SPAN + i * 32, 32), :] = (R.hn[some, :].astype(f32) + qn * w - u * (qn * qn * qn * dot)).astype(bf16)

    in_copy = pltpu.make_async_copy(R.hn.at[SPAN : 2 * SPAN, :], R.grad_in, R.loc.at[6])
    in_copy.start()
    bc_last.wait_send()
    remote(
        R.bfin.at[1 - me.c], R.bfin.at[1 - me.c], R.mate_s.at[2], R.mate_r.at[2], me.mate
    ).wait_recv()
    R.gbc[:, 0:128] = R.bfin[0].astype(f32)
    R.gbc[:, 128:256] = R.bfin[1].astype(f32)
    for d in range(1, 8):
        k, device = me.plane(d)
        remote(R.pv, R.small.at[k], R.ps_s.at[k], R.ps_r.at[k], device).wait()
    dhn.finish(False)
    in_copy.wait()
    out_copy.wait()
    for fin in (wo_sum, x_sum, z_sum, bc_sum, dt_sum):
        for s in stepped(n, fin.finish):
            s()


def shards(
    n,
    hidden_in,
    lengths,
    perm,
    norm_gain,
    w_z,
    w_x,
    w_dt,
    w_bc,
    conv_x,
    conv_x_bias,
    conv_bc,
    conv_bc_bias,
    dt_bias,
    a_log,
    skip_d,
    gate_gain,
    w_out,
    grad_out,
):
    place = lax.axis_index("row") * lax.axis_size("col") + lax.axis_index("col")
    rows, D = hidden_in.shape
    T = rows * 8
    DS, C = w_z.shape
    H = w_dt.shape[1]
    inner = gate_gain.shape[0]
    nb = T // SPAN
    wide_rows = 2 * C + BC + 16

    dealt = jnp.sum(
        jnp.where(perm[:, None] == jnp.arange(lengths.shape[0])[None, :], lengths[None, :], 0), axis=1
    )
    offs = (jnp.cumsum(dealt) - dealt).astype(jnp.int32)
    px = jnp.concatenate(
        [
            conv_x,
            conv_x_bias[None],
            gate_gain[None],
            jnp.repeat(skip_d, inner // skip_d.shape[0])[None],
            jnp.zeros((1, inner), f32),
        ],
        axis=0,
    )
    px = lax.dynamic_slice_in_dim(px, place * C, C, 1).T
    pbc = jnp.concatenate([conv_bc, conv_bc_bias[None], jnp.zeros((3, BC), f32)], axis=0).T
    ph = jnp.stack([dt_bias, -jnp.exp(a_log)], axis=1)
    ph = jnp.pad(lax.dynamic_slice_in_dim(ph, place * H, H, 0), ((0, 8 - H), (0, 6)))
    wdt = jnp.pad(w_dt.astype(bf16).T, ((0, 16 - H), (0, 0)))

    inputs = dict(
        hid=hidden_in,
        gcot=grad_out,
        wz=w_z,
        wx=w_x,
        wbc=w_bc,
        wdt_own=wdt,
        wo=w_out,
        gain=norm_gain[None],
        pxc=px,
        pbcc=pbc,
        ph=ph,
        offs=offs,
    )
    outputs = dict(
        block_out=((rows, D), bf16),
        grad_in=((rows, D), bf16),
        gz=((DS, C), f32),
        gx=((DS, C), f32),
        gbc=((DS, BC), f32),
        gdt_out=((16, DS), f32),
        gwo=((DS, C), f32),
        small=((8, 40, C), f32),
    )
    scratch = dict(
        hn=((T, D), bf16),
        cot=((T, D), bf16),
        wd=((D, 2 * C + BC + 128), bf16),
        wcat=((wide_rows, D), bf16),
        wot=((D, C), bf16),
        wout=((C, D), bf16),
        wdt=((n, 16, DS), bf16),
        pr=((wide_rows, SPAN), f32),
        z=((C, T), bf16),
        xr=((C, T), bf16),
        bcr=((BC, T), bf16),
        ux=((C, T), bf16),
        ubc=((BC, T), bf16),
        dr=((8, T), f32),
        y=((C, T), f32),
        gg=((C, T), bf16),
        dyn=((C, T), bf16),
        dcat=((wide_rows, T), bf16),
        states=((nb, C, STATE), bf16),
        state=((C, STATE), f32),
        gm=((SPAN, SPAN), f32),
        dg=((SPAN, SPAN), f32),
        edy=((C, SPAN), bf16),
        wxd=((C, SPAN), bf16),
        lamb=((C, STATE), bf16),
        tail_x=((C, 128), f32),
        tail_bc=((BC, 128), f32),
        head_x=((3, C, 128), f32),
        head_bc=((3, BC, 128), f32),
        px=((7, C, 128), f32),
        pbc=((5, BC, 128), f32),
        accx=((7, C, 128), f32),
        accbc=((5, BC, 128), f32),
        acch=((2, 8, SPAN), f32),
        sums=((2 * nb, SPAN), f32),
        tot=((2 * nb, SPAN), f32),
        sslot=((8, 2 * nb, SPAN), f32),
        sb=((2, 2, D // 2, SPAN), bf16),
        rb=((4, 2, D // 2, SPAN), bf16),
        da=((D // 2, SPAN), bf16),
        db=((D // 2, SPAN), bf16),
        fx=((2, D // 2, SPAN), bf16),
        fy=((2, D // 2, SPAN), bf16),
        gdt_all=((16, D), bf16),
        gdt=((n, 16, DS), bf16),
        rdt=((n + 1, 16, DS), bf16),
        bsum=((DS, 128), f32),
        bslot=((4, DS, 128), bf16),
        bfin=((2, DS, 128), bf16),
        ng=((1, D), f32),
        sv=((40, C), f32),
        pv=((40, C), f32),
        lslot=((n, 40, C), f32),
    )
    semaphores = dict(
        ag_s=(2, 13),
        ag_r=(2, 13),
        za_s=(5, 2, n - 1),
        za_r=(5, 2, n - 1),
        zr_s=(5, 2, n - 1),
        zr_r=(5, 2, n - 1),
        rs_s=(2, 10),
        rs_r=(2, 10),
        mate_s=(3,),
        mate_r=(3,),
        sum_s=(8,),
        sum_r=(8,),
        ls_s=(n,),
        ls_r=(n,),
        ps_s=(8,),
        ps_r=(8,),
        bc_s=(3,),
        bc_r=(3,),
        loc=(7,),
    )
    names = [*inputs, *outputs, *scratch, *semaphores, "free"]
    vmem = pl.BlockSpec(memory_space=pltpu.VMEM)
    where = {k: pl.BlockSpec(memory_space=pl.ANY) for k in ("gcot", "wz", "wx", "wbc", "block_out", "grad_in")}
    where["offs"] = pl.BlockSpec(memory_space=pltpu.SMEM)
    out = pl.pallas_call(
        functools.partial(kernel, names, n, C, H, float(inner)),
        out_shape=[jax.ShapeDtypeStruct(*s) for s in outputs.values()],
        in_specs=[where.get(k, vmem) for k in inputs],
        out_specs=[where.get(k, vmem) for k in outputs],
        scratch_shapes=[pltpu.VMEM(*s) for s in scratch.values()]
        + [pltpu.SemaphoreType.DMA(s) for s in semaphores.values()]
        + [pltpu.SemaphoreType.REGULAR((5,))],
        compiler_params=pltpu.CompilerParams(
            collective_id=0, has_side_effects=True, vmem_limit_bytes=(64 << 20) - (1 << 18)
        ),
    )(*inputs.values())
    o = types.SimpleNamespace(**dict(zip(outputs, out)))
    own = o.small[:, 0:8, :].transpose(1, 0, 2).reshape(8, inner)
    shared = jnp.sum(o.small[:, 8:24, :], axis=0)
    heads = o.small[:, 24:40, 0].reshape(8, 2, 8)[:, :, 0:H].transpose(1, 0, 2).reshape(2, -1)
    return (
        o.block_out,
        o.grad_in,
        shared[8 : 8 + D // C].reshape(D),
        o.gz,
        o.gx,
        o.gdt_out[0:H].T,
        o.gbc,
        own[0:4],
        own[4],
        shared[0:4, 0:BC],
        shared[4, 0:BC],
        heads[0],
        heads[1],
        jnp.sum(own[6].reshape(skip_d.shape[0], -1), axis=1),
        own[5],
        o.gwo.T,
    )


def solution(mesh):
    assert mesh.shape["row"] == 4 and mesh.shape["col"] == 2
    every = P(("dp", "row", "col"), None)
    weight = P("dp", ("row", "col"))
    out = P(("row", "col"), "dp")
    return jax.shard_map(
        functools.partial(shards, mesh.shape["dp"]),
        mesh=mesh,
        in_specs=(every, P(), P("dp"), P(), weight, weight, weight, P("dp", None))
        + (P(),) * 8
        + (out, every),
        out_specs=(every, every, P(), weight, weight, weight, P("dp", None)) + (P(),) * 8 + (out,),
        check_vma=False,
    )
```

time: 1570 us -> 265 us (0.17); the launches traced: 1550 us -> 263 us
  waiting for transfers between devices: 440 us -> 0 us
  local copies, waits for them, and re-layouts: 369 us -> 21.3 us
  other arithmetic: 318 us -> 2.54 us
  matrix products: 248 us -> 0 us
  Pallas kernels: 0 us -> 239 us
  blocking collectives: 147 us -> 0 us
    dot_general x121 -> x0, matrix products: 248 us -> none  [the longest x24 68.2 us: advance(): inside = jnp.einsum('ijh,jhp->ihp', mixing, x_block, precision=HIGHEST)]
    pallas_call x0 -> x1, Pallas kernels: none -> 239 us  [shards(): pl.pallas_call(functools.partial(kernel, names, n, C, H, float(inner)), o...]
    dynamic_update_slice x36 -> x0, local copies, waits for them, and re-layouts: 165 us -> none  [the longest x32 164 us: ssd_scan(): _, outputs = lax.scan(jax.checkpoint(advance), zero_state, blocks)]
    reduce_scatter x3 -> x0, waiting for transfers between devices: 157 us -> none  [the longest x1 94.9 us: shards(): lax.psum_scatter(lax.dot_general(row_block, in_weight, contract_last, pre...]
    another operation x113 -> x3, other arithmetic: 147 us -> 0.19 us
    psum x1 -> x0, waiting for transfers between devices: 132 us -> none  [shards(): lax.psum((grad_norm_gain, conv_x_grad, conv_xb_grad, pulled[4], pulled[5]...]
    psum x3 -> x0, blocking collectives: 115 us -> none  [the longest x1 88.3 us: shards(): grad_bc = lax.psum(pulled[1], ('row', 'col'))]
    unnamed x17 -> x0, waiting for transfers between devices: 82.3 us -> none
  transfers between devices with their start and end apart: 13 -> 0, of which waited for: 8 -> 0; matrix products, arithmetic and copies ran while one was open for 19% -> 0% of each run, Pallas kernels for 0% -> 0%
where the time goes in v1:
time: 265 us; the launch traced here: 263 us
  Pallas kernels  239 us (90%)
  local copies, waits for them, and re-layouts  21.3 us (8%)
    pallas_call x1, Pallas kernels, shards(): pl.pallas_call(functools.partial(kernel, names, n, C, H, float(inner)), o...  239 us
    unnamed x46, local copies, waits for them, and re-layouts  11.4 us

profile of v1, /device:TPU:8, one launch (start us, length us, event | category | flops | bytes accessed | tf_op | source)
XLA Modules:
  0.0 263.3 jit_solution(7491103817997068679)
XLA Ops:
  0.7 0.6 copy-done.14
  2.3 0.8 copy.56
  3.1 0.7 copy-done.16
  3.8 0.7 copy-done.15
  4.6 0.6 pad.9.refs_10_
  7.0 0.8 copy.53
  7.8 0.6 pad.8.refs_5_
  8.5 0.6 broadcast_in_dim.36.refs_7_
  9.1 238.6 %shard_map.297 = (bf16[256,1536]{1,0:T(8,128)(2,1)}, bf16[256,1536]{1,0:T(8,128)(2,1)}, f32[384,384]{1,0:T(8,128)}, f32[384,384]{1,0:T(8,128)}, f32[384,256]{1,0...) custom-call(bf16[256,1536]{1,0:T(8,128)(2,1)} %refs_0_.1, bf16[256,1536]{1,0:T(8,128)(2,1)} %refs_1_.1, ...), custom_call_target="tpu_custom_call" | custom-call | tf_op jit(solution)/shard_map/pallas_call | solution.py:1086
  247.7 1.0 slice_bitcast_fusion
  248.7 0.6 fusion
  249.4 0.6 reduce_sum.29
  250.0 0.9 slice_reduce_fusion
  251.0 0.6 reshape.78
  251.6 0.6 slice.68
  252.7 0.6 slice.66
  253.4 0.9 slice_reduce_fusion.1
  255.6 1.0 copy.55
  256.7 0.6 slice_bitcast_fusion.1
  257.3 0.9 copy.63
  258.7 0.9 copy.64
  260.0 0.8 copy.65
  261.3 0.8 copy.66
  262.5 0.7 copy.67
  (59 shorter events, 6.8 us)
Async XLA Ops:
  0.6 0.7 copy-start.14
  0.7 0.8 copy-start.6
  1.4 0.7 copy-start.8
  1.5 0.7 copy-start.7
  3.1 0.7 copy-start.16
  3.8 0.7 copy-start.15
  4.6 0.7 copy-start.17
  4.6 0.7 copy-start.18
  5.6 0.7 copy-start.12
  6.2 0.7 copy-start.13
  7.0 0.8 copy-start.9
  7.8 0.7 copy-start.10
  247.7 7.9 %copy-start.4 = (f32[384,384]{1,0:T(8,128)S(1)}, f32[384,384]{1,0:T(8,128)}, u32[]{:S(2)}) copy-start(f32[384,384]{1,0:T(8,128)} %get-tuple-element.31) | copy-start | bytes 1769476
  250.9 6.3 %copy-start.1 = (bf16[256,1536]{1,0:T(8,128)(2,1)S(1)}, bf16[256,1536]{1,0:T(8,128)(2,1)}, u32[]{:S(2)}) copy-start(bf16[256,1536]{1,0:T(8,128)(2,1)} %get-tuple-element.117) | copy-start | bytes 2359300
  255.6 1.1 copy-start.11
  257.3 1.4 copy-start
  258.7 1.3 copy-start.3
  260.0 1.3 copy-start.2
  261.3 1.2 copy-start.5

commit v2 on v1

--- a/solution.py
+++ b/solution.py
@@ -110,18 +110,17 @@
     R.dcat[base + rows.start : base + rows.stop, tok] = out.astype(bf16)
 
 
-def fwd_block(b, R, offs, C, H):
+def scan_block(b, R, offs, C, H):
     p = C // H
     tok = aligned(b * SPAN, SPAN)
-    R.pr[...] = nt(R.wcat[...], R.hn[tok, :])
-    R.z[:, tok] = R.pr[0:C, :].astype(bf16)
-    R.xr[:, tok] = R.pr[C : 2 * C, :].astype(bf16)
-    R.bcr[:, tok] = R.pr[2 * C : 2 * C + BC, :].astype(bf16)
-    dr = R.pr[2 * C + BC : 2 * C + BC + 8, :] + R.ph[:, 0:1]
+    R.pr[...] = nt(R.wcat[C:, :], R.hn[tok, :])
+    R.xr[:, tok] = R.pr[0:C, :].astype(bf16)
+    R.bcr[:, tok] = R.pr[C : C + BC, :].astype(bf16)
+    dr = R.pr[C + BC : C + BC + 8, :] + R.ph[:, 0:1]
     R.dr[:, tok] = dr
     dt = softplus(dr)
     l_row, l_col, e, we, kept, mask, places = decay_terms(b, offs, dt * R.ph[:, 1:2])
-    bcr = R.pr[2 * C : 2 * C + BC, :]
+    bcr = R.pr[C : C + BC, :]
     u = conv_forward(bcr, R.tail_bc[...], R.pbc, slice(0, BC), places).astype(bf16)
     R.tail_bc[...] = bcr[:, 128:]
     R.ubc[:, tok] = u
@@ -129,35 +128,65 @@
     bc = (u * jax.nn.sigmoid(u)).astype(bf16)
     bt, ct = bc[0:STATE, :], bc[STATE:BC, :]
     R.gm[...] = tn(ct, bt) * mask
-    sq = jnp.zeros((1, SPAN), f32)
     for h in range(H):
         rows = slice(h * p, (h + 1) * p)
         hh = slice(h, h + 1)
-        xr = R.pr[C + h * p : C + (h + 1) * p, :]
+        xr = R.pr[rows, :]
         u = conv_forward(xr, R.tail_x[rows, :], R.px, rows, places).astype(bf16)
         R.tail_x[rows, :] = xr[:, 128:]
         R.ux[rows, tok] = u
         u = u.astype(f32)
-        x = u * jax.nn.sigmoid(u)
-        xd = x * dt[hh, :]
+        xd = u * jax.nn.sigmoid(u) * dt[hh, :]
         d = jnp.exp(jnp.minimum(l_col[:, hh] - l_row[hh, :], 0.0))
         mix = (d * R.gm[...]).astype(bf16)
         st = R.state[rows, :]
         stb = st.astype(bf16)
         R.states[b, rows, :] = stb
-        y = nt(xd.astype(bf16), mix) + nn(stb, ct) * e[hh, :]
-        R.y[rows, tok] = y
+        R.y[rows, tok] = nt(xd.astype(bf16), mix) + nn(stb, ct) * e[hh, :]
         R.state[rows, :] = kept[hh, :] * st + nt((xd * we[hh, :]).astype(bf16), bt)
+
+
+def gate_block(b, R, C, H):
+    p = C // H
+    tok = aligned(b * SPAN, SPAN)
+    R.z[:, tok] = nt(R.wcat[0:C, :], R.hn[tok, :]).astype(bf16)
+    sq = jnp.zeros((1, SPAN), f32)
+    for h in range(H):
+        rows = slice(h * p, (h + 1) * p)
+        u = R.ux[rows, tok].astype(f32)
         zz = R.z[rows, tok].astype(f32)
-        gy = (y + wide(R.px, 6, rows) * x) * (zz * jax.nn.sigmoid(zz))
+        yf = R.y[rows, tok] + wide(R.px, 6, rows) * (u * jax.nn.sigmoid(u))
+        gy = yf * (zz * jax.nn.sigmoid(zz))
         sq = sq + jnp.sum(gy * gy, axis=0, keepdims=True)
         R.gg[rows, tok] = (gy * wide(R.px, 5, rows)).astype(bf16)
-    R.sums[pl.ds(b, 1), :] = sq
-
-
-def bwd_block(b, R, offs, C, H, inner):
+    R.sums[0, pl.ds(b, 1), :] = sq
+
+
+def gate_back_block(b, R, C, H, inner):
     p = C // H
-    nb = R.sums.shape[0] // 2
+    tok = aligned(b * SPAN, SPAN)
+    r = lax.rsqrt(R.tot[0, pl.ds(b, 1), :] / inner + EPS)
+    rs = r * r * R.tot[1, pl.ds(b, 1), :] / inner
+    for h in range(H):
+        rows = slice(h * p, (h + 1) * p)
+        u = R.ux[rows, tok].astype(f32)
+        x = u * jax.nn.sigmoid(u)
+        zz = R.z[rows, tok].astype(f32)
+        sz = jax.nn.sigmoid(zz)
+        gate = zz * sz
+        yf = R.y[rows, tok] + wide(R.px, 6, rows) * x
+        gy = yf * gate
+        dyn = R.dyn[rows, tok].astype(f32)
+        R.accx[5, rows, :] += fold(dyn * (gy * r))
+        dgy = (r * wide(R.px, 5, rows)) * dyn - gy * rs
+        R.dcat[rows, tok] = (dgy * yf * (sz + gate * (1.0 - sz))).astype(bf16)
+        dy = dgy * gate
+        R.accx[6, rows, :] += fold(dy * x)
+        R.dyn[rows, tok] = dy.astype(bf16)
+
+
+def bwd_block(b, R, offs, C, H):
+    p = C // H
     tok = aligned(b * SPAN, SPAN)
     v = R.dr[:, tok]
     dt = softplus(v)
@@ -168,8 +197,6 @@
     bc = (ubc * sg).astype(bf16)
     bt, ct = bc[0:STATE, :], bc[STATE:BC, :]
     R.gm[...] = tn(ct, bt) * mask
-    r = lax.rsqrt(R.tot[pl.ds(b, 1), :] / inner + EPS)
-    rs = r * r * r * R.tot[pl.ds(nb + b, 1), :] / inner
     m = [None] + [jnp.where(places >= s, 1.0, 0.0) for s in (1, 2, 3)]
     decays, directs, ends = [], [], []
     for h in range(H):
@@ -179,20 +206,8 @@
         sx = jax.nn.sigmoid(u)
         x = u * sx
         y = R.y[rows, tok]
-        zz = R.z[rows, tok].astype(f32)
-        sz = jax.nn.sigmoid(zz)
-        gate = zz * sz
-        skip = wide(R.px, 6, rows)
-        yf = y + skip * x
-        gy = yf * gate
-        dyn = R.dyn[rows, tok].astype(f32)
-        gyr = gy * r
-        R.accx[5, rows, :] += fold(dyn * gyr)
-        dgy = (r * wide(R.px, 5, rows)) * dyn - gy * rs
-        R.dcat[rows, tok] = (dgy * yf * (sz + gate * (1.0 - sz))).astype(bf16)
-        dy = dgy * gate
-        dyb = dy.astype(bf16)
-        R.accx[6, rows, :] += fold(dy * x)
+        dyb = R.dyn[rows, tok]
+        dy = dyb.astype(f32)
         xd = x * dt[hh, :]
         xdb = xd.astype(bf16)
         d = jnp.exp(jnp.minimum(l_col[:, hh] - l_row[hh, :], 0.0))
@@ -209,7 +224,7 @@
         lb = nn(lamb, bt) * we[hh, :]
         vt = vin + lb
         xlow = xdb.astype(f32)
-        decays.append(jnp.sum(dyb.astype(f32) * y - xlow * vt, axis=0, keepdims=True))
+        decays.append(jnp.sum(dy * y - xlow * vt, axis=0, keepdims=True))
         directs.append(jnp.sum(x * vt, axis=0, keepdims=True))
         through = jnp.sum(lam * stb.astype(f32), axis=0, keepdims=True) * kept[hh, :]
         ends.append(
@@ -221,7 +236,7 @@
         R.wxd[rows, :] = (xd * we[hh, :]).astype(bf16)
         R.lamb[rows, :] = lamb
         R.state[rows, :] = kept[hh, :] * lam + nt(edy, ct)
-        dx = dt[hh, :] * vt + skip * dy
+        dx = dt[hh, :] * vt + wide(R.px, 6, rows) * dy
         du = dx * (sx + x * (1.0 - sx))
         conv_backward(R, R.xr[rows, tok].astype(f32), du, R.px, R.accx, R.head_x, rows, C, tok, m)
     dgm = (R.dg[...] * mask).astype(bf16)
@@ -374,28 +389,16 @@
     def step(self, s):
         me = self.me
         k = me.dp - 1 - s
+        j = me.dp + 1 + s
 
         @pl.when(k >= 0)
         def _():
             self.copy(0, s, k).wait_recv()
 
-            @pl.when(both(me.dp < me.n - 1, s < me.n - 2))
-            def _():
-                self.copy(0, s + 1, k).start()
-
-        j = me.dp + 1 + s
-
         @pl.when(j <= me.n - 1)
         def _():
             self.copy(1, s, j).wait_recv()
 
-            @pl.when(both(me.dp > 0, s < me.n - 2))
-            def _():
-                self.copy(1, s + 1, j).start()
-
-    def finish(self, s):
-        me = self.me
-
         @pl.when(both(me.dp < me.n - 1, me.dp - s >= 0))
         def _():
             self.copy(0, s, me.dp).wait_send()
@@ -403,6 +406,14 @@
         @pl.when(both(me.dp > 0, me.dp + s <= me.n - 1))
         def _():
             self.copy(1, s, me.dp).wait_send()
+
+        @pl.when(both(k >= 0, me.dp < me.n - 1, s < me.n - 2))
+        def _():
+            self.copy(0, s + 1, k).start()
+
+        @pl.when(both(j <= me.n - 1, me.dp > 0, s < me.n - 2))
+        def _():
+            self.copy(1, s + 1, j).start()
 
 
 class LineScatter:
@@ -421,37 +432,36 @@
         (a, i), (b, j) = self.slot(k), self.src(k)
         a[i] = (a[i].astype(f32) + b[j].astype(f32)).astype(bf16)
 
-    def step(self, s):
+    def moves(self, t):
         me, n = self.me, self.me.n
-        k = n - 1 - s
-
-        @pl.when(k > me.dp)
-        def _():
-            @pl.when(me.dp > 0)
-            def _():
-                self.got(0, s, self.slot(k))
-                self.add(k)
-                self.copy(0, s, self.slot(k), self.slot(k)).start()
-
-            @pl.when(me.dp == 0)
-            def _():
-                self.copy(0, s, self.src(k), self.slot(k)).start()
-
-        j = s
-
-        @pl.when(j < me.dp)
-        def _():
-            to = self.slot(jnp.where(j == me.dp - 1, n, j))
-
-            @pl.when(me.dp < n - 1)
-            def _():
-                self.got(1, s, self.slot(j))
-                self.add(j)
-                self.copy(1, s, self.slot(j), to).start()
-
-            @pl.when(me.dp == n - 1)
-            def _():
-                self.copy(1, s, self.src(j), to).start()
+        s, v = t - me.dp, t - (n - 1 - me.dp)
+        return both(s >= 0, n - 1 - s > me.dp), s, n - 1 - s, both(v >= 0, v < me.dp), v, v
+
+    def slot_step(self, t):
+        me, n = self.me, self.me.n
+        to_right, s, k, to_left, v, j = self.moves(t)
+
+        @pl.when(both(to_right, me.dp > 0))
+        def _():
+            self.got(0, s, self.slot(k))
+            self.add(k)
+            self.copy(0, s, self.slot(k), self.slot(k)).start()
+
+        @pl.when(both(to_right, me.dp == 0))
+        def _():
+            self.copy(0, s, self.src(k), self.slot(k)).start()
+
+        to = self.slot(jnp.where(j == me.dp - 1, n, j))
+
+        @pl.when(both(to_left, me.dp < n - 1))
+        def _():
+            self.got(1, v, self.slot(j))
+            self.add(j)
+            self.copy(1, v, self.slot(j), to).start()
+
+        @pl.when(both(to_left, me.dp == n - 1))
+        def _():
+            self.copy(1, v, self.src(j), to).start()
 
     def total(self, put):
         me, n = self.me, self.me.n
@@ -470,16 +480,16 @@
             self.got(1, me.dp, (b, j))
             put(b[j].astype(f32), False)
 
-    def finish(self, s):
-        me, n = self.me, self.me.n
-
-        @pl.when(s < n - 1 - me.dp)
+    def finish(self, t):
+        to_right, s, k, to_left, v, j = self.moves(t)
+
+        @pl.when(to_right)
         def _():
             self.copy(0, s, self.src(0), self.slot(0)).wait_send()
 
-        @pl.when(s < me.dp)
-        def _():
-            self.copy(1, s, self.src(0), self.slot(0)).wait_send()
+        @pl.when(to_left)
+        def _():
+            self.copy(1, v, self.src(0), self.slot(0)).wait_send()
 
 
 class PlaneScatter:
@@ -584,25 +594,35 @@
     return [every] + [lambda: None] * 2
 
 
-def kernel(names, n, C, H, inner, *refs):
+def kernel(names, n, C, H, *refs):
     R = types.SimpleNamespace(**dict(zip(names, refs)))
     me = Place(n)
     T, D = R.hn.shape
+    inner = R.gate.shape[0]
+    heads = R.skip.shape[0]
     nb = T // SPAN
     DS = D // n
     dp = me.dp
-    dt_rows = slice(2 * C + BC, 2 * C + BC + 16)
-    mine = aligned(me.q * SPAN, SPAN)
+    rows = 2 * C + BC + 16
+    dt_rows = slice(2 * C + BC, rows)
     share = lambda k: pl.ds(pl.multiple_of(k * DS, 16), DS)
     dhalf = lambda h: slice(h * (D // 2), (h + 1) * (D // 2))
     half = aligned(2 * C + me.c * 128, 128)
     other = aligned(2 * C + (1 - me.c) * 128, 128)
 
-    barrier = pltpu.get_barrier_semaphore()
-    for d in range(1, 8):
-        pl.semaphore_signal(barrier, 1, device_id=me.plane(d)[1], device_id_type=MESH)
-    for d in range(1, n):
-        pl.semaphore_signal(barrier, 1, device_id=me.line(d)[1], device_id_type=MESH)
+    def over(length):
+        def run(f):
+            pl.loop(0, length)(f)
+
+        return run
+
+    def beside(i, polls):
+        for k, fns in polls.items():
+
+            @pl.when(i == k)
+            def _():
+                for f in fns:
+                    f()
 
     stage = lambda a, z: R.y.at[0:DS, a:z]
     arriving = [
@@ -612,24 +632,30 @@
                 (R.wx, stage(C, 2 * C)),
                 (R.wbc, stage(2 * C, 2 * C + BC)),
                 (R.wz, stage(0, C)),
-                (R.gcot, R.cot.at[mine, :]),
+                (R.gcot, R.cot.at[aligned(me.q * SPAN, SPAN), :]),
             )
         )
     ]
     for copy in arriving:
         copy.start()
-    @pl.loop(0, SPAN // 32)
+    barrier = pltpu.get_barrier_semaphore()
+    for d in range(1, 8):
+        pl.semaphore_signal(barrier, 1, device_id=me.plane(d)[1], device_id_type=MESH)
+    for d in range(1, n):
+        pl.semaphore_signal(barrier, 1, device_id=me.line(d)[1], device_id_type=MESH)
+    R.gains[...] = R.gain[...].reshape(1, D)
+
+    @over(SPAN // 32)
     def _(i):
         u = R.hid[aligned(i * 32, 32), :].astype(f32)
         qn = lax.rsqrt(jnp.mean(u * u, axis=1, keepdims=True) + EPS)
-        R.hn[aligned(me.q * SPAN + i * 32, 32), :] = (u * qn * R.gain[...]).astype(bf16)
-
-    for copy in arriving:
+        R.hn[aligned(me.q * SPAN + i * 32, 32), :] = (u * qn * R.gains[...]).astype(bf16)
+
+    for copy in arriving[:2]:
         copy.wait()
-    R.wd[share(dp), 0 : 2 * C] = R.y[0:DS, 0 : 2 * C].astype(bf16)
+    R.wd[share(dp), C : 2 * C] = R.y[0:DS, C : 2 * C].astype(bf16)
     R.wd[share(dp), half] = R.y[0:DS, half].astype(bf16)
-    R.wot[share(dp), :] = R.wo[...].T.astype(bf16)
-    R.wdt[dp] = R.wdt_own[...]
+    R.wdt[dp] = jnp.concatenate([R.w_dt[...], jnp.zeros((DS, 128 - H), f32)], axis=1).T[0:16, :].astype(bf16)
     pl.semaphore_wait(barrier, 7 + n - 1)
 
     tokens = PlaneGather(me, R.hn, R.ag_s.at[0], R.ag_r.at[0])
@@ -642,97 +668,151 @@
         lambda k: R.wot.at[share(k), :],
     )
     gathers = [LineGather(me, at, R.za_s.at[i], R.za_r.at[i]) for i, at in enumerate(places)]
-    first, wo_gather = gathers[:4], gathers[4]
+    z_gather, wo_gather = gathers[3:]
     tokens.start()
-    for g in first:
+    for g in gathers[:3]:
         g.start()
 
-    for k in range(7):
-        R.px[k] = jnp.broadcast_to(R.pxc[:, k : k + 1], (C, 128))
+    for copy in arriving[2:]:
+        copy.wait()
+    R.wd[share(dp), 0:C] = R.y[0:DS, 0:C].astype(bf16)
+    R.wot[share(dp), :] = R.wo[...].T.astype(bf16)
+    own = aligned(me.q * C, C)
+    taps = [R.conv_x[:, own]]
+    for v in (R.conv_xb, R.gate):
+        R.row[...] = v[...].reshape(1, inner)
+        taps.append(R.row[:, own])
+    taps = jnp.concatenate(taps + [jnp.zeros((2, C), f32)], axis=0).T
+    chan = lax.broadcasted_iota(jnp.int32, (C, heads), 0) // (C // H) + me.q * H
+    pick = chan == lax.broadcasted_iota(jnp.int32, (C, heads), 1)
+    skips = jnp.sum(jnp.where(pick, R.skip[...].reshape(1, heads), 0.0), axis=1, keepdims=True)
+    for k in range(6):
+        R.px[k] = jnp.broadcast_to(taps[:, k : k + 1], (C, 128))
+    R.px[6] = jnp.broadcast_to(skips, (C, 128))
+    taps = jnp.concatenate([R.conv_bc[...], R.conv_bcb[...].reshape(1, BC), jnp.zeros((3, BC), f32)], axis=0).T
     for k in range(5):
-        R.pbc[k] = jnp.broadcast_to(R.pbcc[:, k : k + 1], (BC, 128))
+        R.pbc[k] = jnp.broadcast_to(taps[:, k : k + 1], (BC, 128))
+    head = lax.broadcasted_iota(jnp.int32, (8, heads), 0)
+    pick = (head + me.q * H == lax.broadcasted_iota(jnp.int32, (8, heads), 1)) & (head < H)
+    R.ph[:, 0:1] = jnp.sum(jnp.where(pick, R.dt_bias[...].reshape(1, heads), 0.0), axis=1, keepdims=True)
+    R.ph[:, 1:2] = jnp.sum(
+        jnp.where(pick, -jnp.exp(R.a_log[...].reshape(1, heads)), 0.0), axis=1, keepdims=True
+    )
     for a in (R.tail_bc, R.tail_x, R.state, R.head_x, R.head_bc, R.accx, R.accbc, R.acch, R.sv):
         a[...] = jnp.zeros_like(a)
-    offs = [R.offs[k] for k in range(R.offs.shape[0])]
-
-    line = stepped(n, *[g.step for g in first])
+    offs = [0]
+    for k in range(R.perm.shape[0] - 1):
+        offs.append(offs[-1] + R.lengths[R.perm[k]])
+
+    def line(*fns):
+        if n <= 4:
+            return [lambda s=s: [f(s) for f in fns] for s in range(n - 1)] + [lambda: None] * (4 - n)
+
+        def every():
+            @over(n - 1)
+            def _(s):
+                for f in fns:
+                    f(s)
+
+        return [every] + [lambda: None] * 2
+
+    def prepare(a, z):
+        for k in range(a, z, 128):
+            R.wcat[k : k + 128, :] = R.wd[:, k : k + 128].T
+
+    steps = line(*[g.step for g in gathers[:3]])
     tokens.step1()
-    line[0]()
+    steps[0]()
     tokens.step2()
-    line[1]()
+    steps[1]()
     tokens.step3()
     cots.start()
-    line[2]()
+    steps[2]()
+    z_gather.start()
     bc_swap = remote(R.wd.at[:, half], R.wd.at[:, half], R.mate_s.at[0], R.mate_r.at[0], me.mate)
     bc_swap.start()
-    wo_gather.start()
-    tokens.step4()
-    remote(R.wd.at[:, other], R.wd.at[:, other], R.mate_s.at[0], R.mate_r.at[0], me.mate).wait_recv()
-    bc_swap.wait_send()
-    for s in stepped(n, *[g.finish for g in first]):
-        s()
-    for k in range(0, 2 * C + BC, 256):
-        R.wcat[k : k + 256, :] = R.wd[:, k : k + 256].T
+    prepare(C, 2 * C)
     for k in range(n):
         R.wcat[dt_rows, k * DS : (k + 1) * DS] = R.wdt[k]
     pad = jnp.zeros((112, D), bf16)
     R.wd[:, 2 * C + BC : 2 * C + BC + 128] = jnp.concatenate([R.wcat[dt_rows, :], pad], axis=0).T
-
-    line = stepped(n, wo_gather.step)
-    beside = {3: [cots.step1, line[0]], 5: [line[1]], 6: [cots.step2], 7: [line[2]]}
-
-    @pl.loop(0, nb)
+    remote(R.wd.at[:, other], R.wd.at[:, other], R.mate_s.at[0], R.mate_r.at[0], me.mate).wait_recv()
+    bc_swap.wait_send()
+    prepare(2 * C, 2 * C + BC)
+    tokens.step4()
+
+    steps = line(z_gather.step)
+    polls = {1: [steps[0]], 2: [cots.step1], 4: [steps[1]], 5: [cots.step2], 6: [steps[2], wo_gather.start]}
+
+    @over(nb)
     def _(b):
-        fwd_block(b, R, offs, C, H)
-        for k, fns in beside.items():
-
-            @pl.when(b == min(k, nb - 1))
-            def _():
-                for f in fns:
-                    f()
-
+        scan_block(b, R, offs, C, H)
+        beside(b, polls)
+
+    prepare(0, C)
+
+    @over(nb)
+    def _(b):
+        gate_block(b, R, C, H)
+
+    def share_sums(i):
+        for d in range(1, 8):
+            k, device = me.plane(d)
+            remote(R.sums.at[i], R.sslot.at[i, me.q], R.sum_s.at[i, k], R.sum_r.at[i, me.q], device).start()
+        R.sslot[i, me.q] = R.sums[i]
+
+    def total_sums(i):
+        for d in range(1, 8):
+            k, device = me.plane(d)
+            remote(R.sums.at[i], R.sslot.at[i, k], R.sum_s.at[i, k], R.sum_r.at[i, k], device).wait()
+        total = R.sslot[i, 0]
+        for k in range(1, 8):
+            total = total + R.sslot[i, k]
+        R.tot[i] = total
+
+    share_sums(0)
+    steps = line(wo_gather.step)
+    steps[0]()
     cots.step3()
     cots.step4()
-    for s in stepped(n, wo_gather.finish):
-        s()
+    total_sums(0)
+
+    @over(nb)
+    def _(b):
+        tok = aligned(b * SPAN, SPAN)
+        r = lax.rsqrt(R.tot[0, pl.ds(b, 1), :] / inner + EPS)
+        R.gg[:, tok] = (R.gg[:, tok].astype(f32) * r).astype(bf16)
+
+    @over(D // 256)
+    def _(i):
+        some = aligned(i * 256, 256)
+        R.won[some, :] = nn(R.gg[...], R.cot[:, some]).astype(bf16).T
+
+    steps[1]()
+
+    def scatter(i, src, lanes):
+        slot = lambda k: (R.cot, (share(k), slice(*lanes)))
+        return LineScatter(me, src, slot, R.zr_s.at[i], R.zr_r.at[i])
+
+    wo_sum = scatter(0, lambda k: (R.won, (share(k), slice(0, C))), (2 * C + 128, 3 * C + 128))
+    x_sum = scatter(1, lambda k: (R.wd, (share(k), slice(C, 2 * C))), (C, 2 * C))
+    z_sum = scatter(2, lambda k: (R.wot, (share(k), slice(0, C))), (0, C))
+    bc_sum = scatter(3, lambda k: (R.wd, (share(k), half)), (2 * C, 2 * C + 128))
+    dt_sum = LineScatter(
+        me, lambda k: (R.gdt, (k,)), lambda k: (R.rdt, (k,)), R.zr_s.at[4], R.zr_r.at[4]
+    )
+    steps[2]()
     for k in range(0, D, 256):
         R.wout[:, k : k + 256] = R.wot[k : k + 256, :].T
 
-    @pl.loop(0, nb)
+    @over(nb)
     def _(b):
         tok = aligned(b * SPAN, SPAN)
         dyn = nt(R.wout[...], R.cot[tok, :])
         R.dyn[:, tok] = dyn.astype(bf16)
-        R.sums[pl.ds(nb + b, 1), :] = jnp.sum(dyn * R.gg[:, tok].astype(f32), axis=0, keepdims=True)
-
-    for d in range(1, 8):
-        k, device = me.plane(d)
-        remote(R.sums, R.sslot.at[me.q], R.sum_s.at[k], R.sum_r.at[me.q], device).start()
-    R.sslot[me.q] = R.sums[...]
-
-    mixed = PlaneScatter(
-        me, R, R.rs_s.at[0], R.rs_r.at[0], lambda k, h: nn(R.wot[dhalf(h), :], R.gg[:, aligned(k * SPAN, SPAN)]), False
-    )
-    mixed.first()
-    mixed.second()
-    for d in range(1, 8):
-        k, device = me.plane(d)
-        remote(R.sums, R.sslot.at[k], R.sum_s.at[k], R.sum_r.at[k], device).wait()
-    total = R.sslot[0]
-    for k in range(1, 8):
-        total = total + R.sslot[k]
-    R.tot[...] = total
-
-    @pl.loop(0, nb)
-    def _(b):
-        tok = aligned(b * SPAN, SPAN)
-        r = lax.rsqrt(R.tot[pl.ds(b, 1), :] / inner + EPS)
-        R.gg[:, tok] = (R.gg[:, tok].astype(f32) * r).astype(bf16)
-
-    @pl.loop(0, D // 256)
-    def _(i):
-        some = aligned(i * 256, 256)
-        R.wot[some, :] = nn(R.gg[...], R.cot[:, some]).astype(bf16).T
+        R.sums[1, pl.ds(b, 1), :] = jnp.sum(dyn * R.gg[:, tok].astype(f32), axis=0, keepdims=True)
+
+    share_sums(1)
 
     @pl.when(dp < n - 1)
     def _():
@@ -742,6 +822,16 @@
     def _():
         pl.semaphore_signal(R.free.at[4], 1, device_id=me.left(), device_id_type=MESH)
 
+    mixed = PlaneScatter(
+        me,
+        R,
+        R.rs_s.at[0],
+        R.rs_r.at[0],
+        lambda k, h: nn(R.wot[dhalf(h), :], R.gg[:, aligned(k * SPAN, SPAN)]),
+        False,
+    )
+    mixed.first()
+
     @pl.when(dp > 0)
     def _():
         pl.semaphore_wait(R.free.at[3], 1)
@@ -750,17 +840,31 @@
     def _():
         pl.semaphore_wait(R.free.at[4], 1)
 
-    def scatter(i, src, lanes):
-        slot = lambda k: (R.cot, (share(k), slice(*lanes)))
-        return LineScatter(me, src, slot, R.zr_s.at[i], R.zr_r.at[i])
-
-    wo_sum = scatter(0, lambda k: (R.wot, (share(k), slice(0, C))), (2 * C + 128, 3 * C + 128))
-    x_sum = scatter(1, lambda k: (R.wd, (share(k), slice(C, 2 * C))), (C, 2 * C))
-    z_sum = scatter(2, lambda k: (R.wd, (share(k), slice(0, C))), (0, C))
-    bc_sum = scatter(3, lambda k: (R.wd, (share(k), half)), (2 * C, 2 * C + 128))
-    dt_sum = LineScatter(
-        me, lambda k: (R.gdt, (k,)), lambda k: (R.rdt, (k,)), R.zr_s.at[4], R.zr_r.at[4]
-    )
+    wo_steps = line(wo_sum.slot_step)
+    wo_steps[0]()
+    mixed.second()
+    total_sums(1)
+
+    @over(nb)
+    def _(b):
+        gate_back_block(b, R, C, H, inner)
+
+    def weight_grad(a, z, dst, at):
+        @over(D // 256)
+        def _(i):
+            some = aligned(i * 256, 256)
+            g = nn(R.dcat[a:z, :], R.hn[:, some])
+            R.ng[:, some] += jnp.sum(g * R.wcat[a:z, some].astype(f32), axis=0, keepdims=True)
+            g = g.astype(bf16)
+            if z - a > 256:
+                R.gdt_all[:, some] = g[z - a - 16 : z - a]
+            w = min(z - a, 256)
+            dst[some, at : at + w] = g[0:w].T
+
+    R.ng[...] = jnp.zeros_like(R.ng)
+    weight_grad(0, 256, R.wot, 0)
+    weight_grad(256, C, R.wot, 256)
+    wo_steps[1]()
 
     def put(ref):
         def f(v, new):
@@ -774,31 +878,28 @@
     out_copy = pltpu.make_async_copy(R.wout.at[0:SPAN, :], R.block_out, R.loc.at[5])
 
     def finish_mixed():
-        r = lax.rsqrt(R.tot[pl.ds(me.q, 1), :] / inner + EPS)
-
         def put(k, v):
             cols = aligned(k * 128, 128)
-            R.wout[0:SPAN, cols] = (R.hid[:, cols].astype(f32) + (v * r).T).astype(bf16)
+            R.wout[0:SPAN, cols] = (R.hid[:, cols].astype(f32) + v.T).astype(bf16)
 
         mixed.total(put)
         out_copy.start()
         mixed.finish(True)
 
     R.state[...] = jnp.zeros_like(R.state)
-    line = stepped(n, wo_sum.step)
-    beside = {1: [mixed.relay, line[0]], 3: [line[1]], 5: [line[2]], 6: [finish_mixed]}
-
-    @pl.loop(0, nb)
+    z_steps = line(z_sum.slot_step)
+    polls = {
+        0: [mixed.relay],
+        1: [wo_steps[2], z_steps[0]],
+        4: [z_steps[1], finish_mixed],
+        7: [z_steps[2]],
+    }
+
+    @over(nb)
     def _(i):
-        bwd_block(nb - 1 - i, R, offs, C, H, inner)
-        for k, fns in beside.items():
-
-            @pl.when(i == min(k, nb - 1))
-            def _():
-                for f in fns:
-                    f()
-
-    rows = 2 * C + BC + 16
+        bwd_block(nb - 1 - i, R, offs, C, H)
+        beside(i, polls)
+
     dhn = PlaneScatter(
         me,
         R,
@@ -810,53 +911,41 @@
     dhn.first()
     dhn.second()
 
-    def weight_grad(a, z):
-        @pl.loop(0, D // 256)
-        def _(i):
-            some = aligned(i * 256, 256)
-            g = nn(R.dcat[a:z, :], R.hn[:, some])
-            R.ng[:, some] += jnp.sum(g * R.wcat[a:z, some].astype(f32), axis=0, keepdims=True)
-            g = g.astype(bf16)
-            R.wd[some, a : a + 256] = g[0:256].T
-            if z - a > 256:
-                R.gdt_all[:, some] = g[256:272]
-
-    R.ng[...] = jnp.zeros_like(R.ng)
-    weight_grad(2 * C, rows)
+    weight_grad(2 * C - 256, 2 * C, R.wd, 2 * C - 256)
+    weight_grad(C, 2 * C - 256, R.wd, C)
+    x_steps = line(x_sum.slot_step)
+    x_steps[0]()
+    weight_grad(2 * C, rows, R.wd, 2 * C)
     for k in range(n):
         R.gdt[k] = R.gdt_all[:, k * DS : (k + 1) * DS]
     bx = R.cot.at[0:D, 3 * C + 128 : 3 * C + 256]
     bc_pair = remote(R.wd.at[:, other], bx, R.mate_s.at[1], R.mate_r.at[1], me.mate)
     bc_pair.start()
-    for a in (2 * C - 256, 2 * C - 512):
-        weight_grad(a, a + 256)
-    bc_pair.wait()
-    R.wd[:, half] = (R.wd[:, half].astype(f32) + bx[...].astype(f32)).astype(bf16)
-    line = stepped(n, x_sum.step, bc_sum.step, dt_sum.step)
-    line[0]()
     dhn.relay()
-    for a in range(2 * C - 768, -1, -256):
-        weight_grad(a, a + 256)
-    zline = stepped(n, z_sum.step)
-    zline[0]()
 
     ax = [jnp.sum(R.accx[k], axis=1, keepdims=True) for k in range(7)]
     ab = [jnp.sum(R.accbc[k], axis=1, keepdims=True) for k in range(5)]
-    R.sv[0:8, :] = jnp.concatenate(ax + [jnp.zeros((C, 1), f32)], axis=1).T
+    ah = [jnp.sum(R.acch[k], axis=1, keepdims=True) for k in range(2)]
+    p = C // H
+    ah += [jnp.sum(ax[6][h * p : (h + 1) * p], axis=0, keepdims=True) for h in range(H)]
+    ah = jnp.concatenate(ah + [jnp.zeros((8 - H, 1), f32)], axis=0)
+    R.sv[0:8, :] = jnp.concatenate(ax[:6] + [jnp.zeros((C, 2), f32)], axis=1).T
+    R.sv[6:7, 0:128] = jnp.concatenate(
+        [jnp.broadcast_to(ah, (24, 128)), jnp.zeros((104, 128), f32)], axis=0
+    ).T[0:1, :]
     R.sv[8:16, 0:BC] = jnp.concatenate(ab + [jnp.zeros((BC, 3), f32)], axis=1).T
-    ng = R.ng[...] / R.gain[...]
+    ng = R.ng[...] / R.gains[...]
     for k in range(D // C):
         R.sv[16 + k : 17 + k, :] = ng[:, k * C : (k + 1) * C]
-    for k in range(2):
-        R.sv[24 + 8 * k : 32 + 8 * k, 0:128] = jnp.broadcast_to(
-            jnp.sum(R.acch[k], axis=1, keepdims=True), (8, 128)
-        )
     for d in range(1, n):
         k, device = me.line(d)
         remote(R.sv, R.lslot.at[dp], R.ls_s.at[k], R.ls_r.at[dp], device).start()
     R.lslot[dp] = R.sv[...]
-    line[1]()
-    zline[1]()
+    x_steps[1]()
+    bc_pair.wait()
+    R.wd[:, half] = (R.wd[:, half].astype(f32) + bx[...].astype(f32)).astype(bf16)
+    bc_steps = line(bc_sum.slot_step, dt_sum.slot_step)
+    bc_steps[0]()
     for d in range(1, n):
         k, device = me.line(d)
         remote(R.sv, R.lslot.at[k], R.ls_s.at[k], R.ls_r.at[k], device).wait()
@@ -868,10 +957,12 @@
         k, device = me.plane(d)
         remote(R.pv, R.small.at[me.q], R.ps_s.at[k], R.ps_r.at[me.q], device).start()
     R.small[me.q] = total
-    line[2]()
-    zline[2]()
-
-    x_sum.total(put(R.gx))
+    bc_steps[1]()
+    x_steps[2]()
+    bc_steps[2]()
+
+    wo_sum.total(put(R.gwo))
+    z_sum.total(put(R.gz))
     bc_sum.total(put(R.bsum))
     j = me.x * 2 + me.y
     R.bslot[j] = R.bsum[...].astype(bf16)
@@ -881,9 +972,8 @@
     ):
         remote(R.bslot.at[j], R.bslot.at[j], R.bc_s.at[i], R.bc_r.at[i], device).start()
         crossing.append(remote(R.bslot.at[k], R.bslot.at[k], R.bc_s.at[i], R.bc_r.at[i], device))
-    z_sum.total(put(R.gz))
+    x_sum.total(put(R.gx))
     dt_sum.total(put(R.gdt_out))
-    wo_sum.total(put(R.gwo))
     for c in crossing:
         c.wait()
     v = R.bslot[0].astype(f32)
@@ -895,20 +985,23 @@
 
     cot_again = pltpu.make_async_copy(R.gcot, R.hn.at[0:SPAN, :], R.loc.at[4])
     cot_again.start()
+
     def put_dh(k, v):
         R.y[0:SPAN, aligned(k * 128, 128)] = v.T
 
     dhn.total(put_dh)
     cot_again.wait()
 
-    @pl.loop(0, SPAN // 32)
+    @over(SPAN // 32)
     def _(i):
         some = aligned(i * 32, 32)
         u = R.hid[some, :].astype(f32)
         qn = lax.rsqrt(jnp.mean(u * u, axis=1, keepdims=True) + EPS)
-        w = R.y[some, 0:D] * R.gain[...]
+        w = R.y[some, 0:D] * R.gains[...]
         dot = jnp.sum(w * u, axis=1, keepdims=True) / D
-        R.hn[aligned(SPAN + i * 32, 32), :] = (R.hn[some, :].astype(f32) + qn * w - u * (qn * qn * qn * dot)).astype(bf16)
+        R.hn[aligned(SPAN + i * 32, 32), :] = (
+            R.hn[some, :].astype(f32) + qn * w - u * (qn * qn * qn * dot)
+        ).astype(bf16)
 
     in_copy = pltpu.make_async_copy(R.hn.at[SPAN : 2 * SPAN, :], R.grad_in, R.loc.at[6])
     in_copy.start()
@@ -922,11 +1015,49 @@
         k, device = me.plane(d)
         remote(R.pv, R.small.at[k], R.ps_s.at[k], R.ps_r.at[k], device).wait()
     dhn.finish(False)
+    for fin in (wo_sum, x_sum, z_sum, bc_sum, dt_sum):
+        for s in line(fin.finish):
+            s()
     in_copy.wait()
     out_copy.wait()
-    for fin in (wo_sum, x_sum, z_sum, bc_sum, dt_sum):
-        for s in stepped(n, fin.finish):
-            s()
+
+
+def unpack(names, C, H, *refs):
+    R = types.SimpleNamespace(**dict(zip(names, refs)))
+    big = [
+        pltpu.make_async_copy(a, b, R.sem.at[i])
+        for i, (a, b) in enumerate(
+            (
+                (R.block_out, R.o_block),
+                (R.grad_in, R.o_grad),
+                (R.gz, R.o_z),
+                (R.gx, R.o_x),
+                (R.gbc, R.o_bc),
+            )
+        )
+    ]
+    for copy in big:
+        copy.start()
+    R.o_wo[...] = R.gwo[...].T
+    DS = R.gdt_out.shape[1]
+    R.o_dt[...] = jnp.concatenate([R.gdt_out[...], jnp.zeros((112, DS), f32)], axis=0).T[:, 0:H]
+    row = lambda k: jnp.concatenate([R.small[q, k : k + 1, :] for q in range(8)], axis=1)
+    for k in range(KERNEL):
+        R.o_cx[k : k + 1, :] = row(k)
+    R.o_cxb[...] = row(4).reshape(8 * C)
+    R.o_gate[...] = row(5).reshape(8 * C)
+    for ref, at in ((R.o_dtb, 0), (R.o_alog, 8), (R.o_skip, 16)):
+        v = jnp.concatenate([R.small[q, 6:7, at : at + H] for q in range(8)], axis=1)
+        ref[...] = v.reshape(8 * H)
+    total = R.small[0, 8:24, :]
+    for q in range(1, 8):
+        total = total + R.small[q, 8:24, :]
+    R.o_cbc[...] = total[0:KERNEL, 0:BC]
+    R.o_cbcb[...] = total[4:5, 0:BC].reshape(BC)
+    D = R.o_ng.shape[0]
+    R.o_ng[...] = jnp.concatenate([total[8 + k : 9 + k, :] for k in range(D // C)], axis=1).reshape(D)
+    for copy in big:
+        copy.wait()
 
 
 def shards(
@@ -950,7 +1081,6 @@
     w_out,
     grad_out,
 ):
-    place = lax.axis_index("row") * lax.axis_size("col") + lax.axis_index("col")
     rows, D = hidden_in.shape
     T = rows * 8
     DS, C = w_z.shape
@@ -958,40 +1088,25 @@
     inner = gate_gain.shape[0]
     nb = T // SPAN
     wide_rows = 2 * C + BC + 16
-
-    dealt = jnp.sum(
-        jnp.where(perm[:, None] == jnp.arange(lengths.shape[0])[None, :], lengths[None, :], 0), axis=1
-    )
-    offs = (jnp.cumsum(dealt) - dealt).astype(jnp.int32)
-    px = jnp.concatenate(
-        [
-            conv_x,
-            conv_x_bias[None],
-            gate_gain[None],
-            jnp.repeat(skip_d, inner // skip_d.shape[0])[None],
-            jnp.zeros((1, inner), f32),
-        ],
-        axis=0,
-    )
-    px = lax.dynamic_slice_in_dim(px, place * C, C, 1).T
-    pbc = jnp.concatenate([conv_bc, conv_bc_bias[None], jnp.zeros((3, BC), f32)], axis=0).T
-    ph = jnp.stack([dt_bias, -jnp.exp(a_log)], axis=1)
-    ph = jnp.pad(lax.dynamic_slice_in_dim(ph, place * H, H, 0), ((0, 8 - H), (0, 6)))
-    wdt = jnp.pad(w_dt.astype(bf16).T, ((0, 16 - H), (0, 0)))
-
     inputs = dict(
         hid=hidden_in,
         gcot=grad_out,
         wz=w_z,
         wx=w_x,
         wbc=w_bc,
-        wdt_own=wdt,
+        w_dt=w_dt,
         wo=w_out,
-        gain=norm_gain[None],
-        pxc=px,
-        pbcc=pbc,
-        ph=ph,
-        offs=offs,
+        gain=norm_gain,
+        conv_x=conv_x,
+        conv_xb=conv_x_bias,
+        conv_bc=conv_bc,
+        conv_bcb=conv_bc_bias,
+        dt_bias=dt_bias,
+        a_log=a_log,
+        skip=skip_d,
+        gate=gate_gain,
+        lengths=lengths,
+        perm=perm,
     )
     outputs = dict(
         block_out=((rows, D), bf16),
@@ -1001,7 +1116,7 @@
         gbc=((DS, BC), f32),
         gdt_out=((16, DS), f32),
         gwo=((DS, C), f32),
-        small=((8, 40, C), f32),
+        small=((8, 24, C), f32),
     )
     scratch = dict(
         hn=((T, D), bf16),
@@ -1010,8 +1125,9 @@
         wcat=((wide_rows, D), bf16),
         wot=((D, C), bf16),
         wout=((C, D), bf16),
+        won=((D, C), bf16),
         wdt=((n, 16, DS), bf16),
-        pr=((wide_rows, SPAN), f32),
+        pr=((C + BC + 16, SPAN), f32),
         z=((C, T), bf16),
         xr=((C, T), bf16),
         bcr=((BC, T), bf16),
@@ -1035,12 +1151,15 @@
         head_bc=((3, BC, 128), f32),
         px=((7, C, 128), f32),
         pbc=((5, BC, 128), f32),
+        ph=((8, 128), f32),
+        row=((1, inner), f32),
+        gains=((1, D), f32),
         accx=((7, C, 128), f32),
         accbc=((5, BC, 128), f32),
         acch=((2, 8, SPAN), f32),
-        sums=((2 * nb, SPAN), f32),
-        tot=((2 * nb, SPAN), f32),
-        sslot=((8, 2 * nb, SPAN), f32),
+        sums=((2, nb, SPAN), f32),
+        tot=((2, nb, SPAN), f32),
+        sslot=((2, 8, nb, SPAN), f32),
         sb=((2, 2, D // 2, SPAN), bf16),
         rb=((4, 2, D // 2, SPAN), bf16),
         da=((D // 2, SPAN), bf16),
@@ -1054,9 +1173,9 @@
         bslot=((4, DS, 128), bf16),
         bfin=((2, DS, 128), bf16),
         ng=((1, D), f32),
-        sv=((40, C), f32),
-        pv=((40, C), f32),
-        lslot=((n, 40, C), f32),
+        sv=((24, C), f32),
+        pv=((24, C), f32),
+        lslot=((n, 24, C), f32),
     )
     semaphores = dict(
         ag_s=(2, 13),
@@ -1069,8 +1188,8 @@
         rs_r=(2, 10),
         mate_s=(3,),
         mate_r=(3,),
-        sum_s=(8,),
-        sum_r=(8,),
+        sum_s=(2, 8),
+        sum_r=(2, 8),
         ls_s=(n,),
         ls_r=(n,),
         ps_s=(8,),
@@ -1081,10 +1200,12 @@
     )
     names = [*inputs, *outputs, *scratch, *semaphores, "free"]
     vmem = pl.BlockSpec(memory_space=pltpu.VMEM)
-    where = {k: pl.BlockSpec(memory_space=pl.ANY) for k in ("gcot", "wz", "wx", "wbc", "block_out", "grad_in")}
-    where["offs"] = pl.BlockSpec(memory_space=pltpu.SMEM)
+    hbm = pl.BlockSpec(memory_space=pl.ANY)
+    smem = pl.BlockSpec(memory_space=pltpu.SMEM)
+    where = {k: hbm for k in ("gcot", "wz", "wx", "wbc", "block_out", "grad_in")}
+    where.update(lengths=smem, perm=smem)
     out = pl.pallas_call(
-        functools.partial(kernel, names, n, C, H, float(inner)),
+        functools.partial(kernel, names, n, C, H),
         out_shape=[jax.ShapeDtypeStruct(*s) for s in outputs.values()],
         in_specs=[where.get(k, vmem) for k in inputs],
         out_specs=[where.get(k, vmem) for k in outputs],
@@ -1095,28 +1216,34 @@
             collective_id=0, has_side_effects=True, vmem_limit_bytes=(64 << 20) - (1 << 18)
         ),
     )(*inputs.values())
-    o = types.SimpleNamespace(**dict(zip(outputs, out)))
-    own = o.small[:, 0:8, :].transpose(1, 0, 2).reshape(8, inner)
-    shared = jnp.sum(o.small[:, 8:24, :], axis=0)
-    heads = o.small[:, 24:40, 0].reshape(8, 2, 8)[:, :, 0:H].transpose(1, 0, 2).reshape(2, -1)
-    return (
-        o.block_out,
-        o.grad_in,
-        shared[8 : 8 + D // C].reshape(D),
-        o.gz,
-        o.gx,
-        o.gdt_out[0:H].T,
-        o.gbc,
-        own[0:4],
-        own[4],
-        shared[0:4, 0:BC],
-        shared[4, 0:BC],
-        heads[0],
-        heads[1],
-        jnp.sum(own[6].reshape(skip_d.shape[0], -1), axis=1),
-        own[5],
-        o.gwo.T,
+
+    results = dict(
+        o_block=((rows, D), bf16),
+        o_grad=((rows, D), bf16),
+        o_ng=((D,), f32),
+        o_z=((DS, C), f32),
+        o_x=((DS, C), f32),
+        o_dt=((DS, H), f32),
+        o_bc=((DS, BC), f32),
+        o_cx=((KERNEL, inner), f32),
+        o_cxb=((inner,), f32),
+        o_cbc=((KERNEL, BC), f32),
+        o_cbcb=((BC,), f32),
+        o_dtb=(dt_bias.shape, f32),
+        o_alog=(a_log.shape, f32),
+        o_skip=(skip_d.shape, f32),
+        o_gate=((inner,), f32),
+        o_wo=((C, DS), f32),
     )
+    copied = ("o_block", "o_grad", "o_z", "o_x", "o_bc")
+    place = lambda k: hbm if k in copied else vmem
+    return pl.pallas_call(
+        functools.partial(unpack, [*outputs, *results, "sem"], C, H),
+        out_shape=[jax.ShapeDtypeStruct(*s) for s in results.values()],
+        in_specs=[place(k) for k in outputs],
+        out_specs=[place(k) for k in results],
+        scratch_shapes=[pltpu.SemaphoreType.DMA((5,))],
+    )(*out)
 
 
 def solution(mesh):

time: 265 us -> 197 us (0.74)
  Pallas kernels: 239 us -> 192 us
  local copies, waits for them, and re-layouts: 21.3 us -> 3.16 us
    pallas_call x1 -> x2, Pallas kernels: 239 us -> 192 us  [the longest x1 187 us: shards(): pl.pallas_call(functools.partial(kernel, names, n, C, H), out_shape=[jax....]
    unnamed x46 -> x1, local copies, waits for them, and re-layouts: 11.4 us -> 1.53 us
    slice x7 -> x0, local copies, waits for them, and re-layouts: 3.38 us -> none  [the longest x1 0.93 us: shards(): o.small[:, 24:40, 0].reshape(8, 2, 8)[:, :, 0:H].transpose(1, 0, 2)]
where the time goes in v2:
time: 197 us; the launch traced here: 195 us
  Pallas kernels  192 us (97%)
  local copies, waits for them, and re-layouts  3.16 us (2%)
    pallas_call x1, Pallas kernels, shards(): pl.pallas_call(functools.partial(kernel, names, n, C, H), out_shape=[jax....  187 us
    pallas_call x1, Pallas kernels, shards(): pl.pallas_call(functools.partial(unpack, [*outputs, *results, 'sem'], C,...  4.74 us

profile of v2, /device:TPU:8, one launch (start us, length us, event | category | flops | bytes accessed | tf_op | source)
XLA Modules:
  0.0 195.5 jit_solution(6998858195624149595)
XLA Ops:
  0.6 1.5 copy.34.refs_5_
  2.2 186.9 %shard_map.297 = (bf16[256,1536]{1,0:T(8,128)(2,1)}, bf16[256,1536]{1,0:T(8,128)(2,1)}, f32[384,384]{1,0:T(8,128)}, f32[384,384]{1,0:T(8,128)}, f32[384,256]{1,0...) custom-call(bf16[256,1536]{1,0:T(8,128)(2,1)} %refs_0_.1, bf16[256,1536]{1,0:T(8,128)(2,1)} %refs_1_.1, ...), custom_call_target="tpu_custom_call" | custom-call | tf_op jit(solution)/shard_map/pallas_call | solution.py:1207
  189.1 4.7 %shard_map.298 = (bf16[256,1536]{1,0:T(8,128)(2,1)}, bf16[256,1536]{1,0:T(8,128)(2,1)}, f32[1536]{0:T(1024)}, f32[384,384]{1,0:T(8,128)}, f32[384,384]{1,0:T(8,1...) custom-call(bf16[256,1536]{1,0:T(8,128)(2,1)} %get-tuple-element.24., ...), custom_call_target="tpu_custom_call" | custom-call | tf_op jit(solution)/shard_map/pallas_call | solution.py:1240
  193.8 1.6 copy.35

commit v3 on v2

--- a/solution.py
+++ b/solution.py
@@ -16,6 +16,7 @@
 EPS = 1e-5
 f32, bf16 = jnp.float32, jnp.bfloat16
 MESH = pl.DeviceIdType.MESH
+LITTLE = ("w_dt", "gain", "conv_x", "conv_xb", "conv_bc", "conv_bcb", "dt_bias", "a_log", "skip", "gate")
 
 
 def nt(a, b):
@@ -55,7 +56,7 @@
     return (i >= j).astype(bf16)
 
 
-def decay_terms(b, offs, da):
+def decay_terms(b, offs, da, flip=False):
     first = b * SPAN
     row = first + lax.broadcasted_iota(jnp.int32, (1, SPAN), 1)
     col = first + lax.broadcasted_iota(jnp.int32, (SPAN, 1), 0)
@@ -74,7 +75,8 @@
     e = jnp.where(beg_r < first, jnp.exp(l_row), 0.0)
     we = jnp.where(beg_r == end_b, jnp.exp(last - l_row), 0.0)
     kept = jnp.where(end_b < first, jnp.exp(last), 0.0)
-    mask = jnp.where((beg_r == beg_c) & (row <= col), 1.0, 0.0)
+    order = (col <= row) if flip else (row <= col)
+    mask = jnp.where((beg_r == beg_c) & order, 1.0, 0.0)
     return l_row, l_col, e, we, kept, mask, row - beg_r
 
 
@@ -119,7 +121,7 @@
     dr = R.pr[C + BC : C + BC + 8, :] + R.ph[:, 0:1]
     R.dr[:, tok] = dr
     dt = softplus(dr)
-    l_row, l_col, e, we, kept, mask, places = decay_terms(b, offs, dt * R.ph[:, 1:2])
+    l_row, l_col, e, we, kept, mask, places = decay_terms(b, offs, dt * R.ph[:, 1:2], True)
     bcr = R.pr[C : C + BC, :]
     u = conv_forward(bcr, R.tail_bc[...], R.pbc, slice(0, BC), places).astype(bf16)
     R.tail_bc[...] = bcr[:, 128:]
@@ -127,7 +129,7 @@
     u = u.astype(f32)
     bc = (u * jax.nn.sigmoid(u)).astype(bf16)
     bt, ct = bc[0:STATE, :], bc[STATE:BC, :]
-    R.gm[...] = tn(ct, bt) * mask
+    R.gm[...] = tn(bt, ct) * mask
     for h in range(H):
         rows = slice(h * p, (h + 1) * p)
         hh = slice(h, h + 1)
@@ -137,12 +139,12 @@
         R.ux[rows, tok] = u
         u = u.astype(f32)
         xd = u * jax.nn.sigmoid(u) * dt[hh, :]
-        d = jnp.exp(jnp.minimum(l_col[:, hh] - l_row[hh, :], 0.0))
+        d = jnp.exp(jnp.minimum(l_row[hh, :] - l_col[:, hh], 0.0))
         mix = (d * R.gm[...]).astype(bf16)
         st = R.state[rows, :]
         stb = st.astype(bf16)
         R.states[b, rows, :] = stb
-        R.y[rows, tok] = nt(xd.astype(bf16), mix) + nn(stb, ct) * e[hh, :]
+        R.y[rows, tok] = nn(xd.astype(bf16), mix) + nn(stb, ct) * e[hh, :]
         R.state[rows, :] = kept[hh, :] * st + nt((xd * we[hh, :]).astype(bf16), bt)
 
 
@@ -501,52 +503,63 @@
     def copy(self, i, src, dst, device):
         return remote(src, dst, self.send.at[i], self.recv.at[i], device)
 
-    def first(self):
+    def block(self, t):
+        me = self.me
+        dx, dy = 1 - t // 2, 1 - t % 2
+        return me.x + dx * (1 - 2 * me.x), me.y + dy * (1 - 2 * me.y)
+
+    def for_mate(self, t):
         me, R = self.me, self.R
+        xx, yy = self.block(t)
+        k = me.index(xx, 1 - me.c, yy)
+        slot = R.sb.at[t % 2]
+
+        @pl.when(t >= 2)
+        def _():
+            self.copy(t - 2, slot, slot, me.mate).wait_send()
+
+        R.sb[t % 2, 0] = self.part(k, 0).astype(bf16)
+        R.sb[t % 2, 1] = self.part(k, 1).astype(bf16)
+        self.copy(t, slot, R.rb.at[xx * 2 + yy], me.mate).start()
+
+    def for_this(self, t):
+        me, R = self.me, self.R
+        xx, yy = self.block(t)
+        j = xx * 2 + yy
+        k = me.index(xx, me.c, yy)
+        self.copy(t, R.rb.at[j], R.rb.at[j], me.mate).wait_recv()
+        R.rb[j, 0] = (self.part(k, 0) + R.rb[j, 0].astype(f32)).astype(bf16)
+        R.rb[j, 1] = (self.part(k, 1) + R.rb[j, 1].astype(f32)).astype(bf16)
+
+        @pl.when(t == 0)
+        def _():
+            self.copy(4, R.rb.at[self.jd, 0], R.da, me.xn).start()
+            self.copy(5, R.rb.at[self.jd, 1], R.db, me.yn).start()
+
+        @pl.when(t == 1)
+        def _():
+            self.copy(6, R.rb.at[self.jx, 0], R.fx.at[0], me.xn).start()
+
+        @pl.when(t == 2)
+        def _():
+            self.copy(9, R.rb.at[self.jy, 1], R.fy.at[1], me.yn).start()
+
+    def blocks(self, beside):
         if self.credit:
-            pl.semaphore_wait(R.free.at[0], 1)
-
-        @pl.loop(0, 4)
-        def _(j):
-            k = me.index(j // 2, 1 - me.c, j % 2)
-
-            @pl.when(j >= 2)
+            for i in (1, 2):
+                pl.semaphore_wait(self.R.free.at[i], 1)
+
+        @pl.loop(0, 5)
+        def _(t):
+            @pl.when(t < 4)
             def _():
-                self.copy(j - 2, R.sb.at[j % 2], R.rb.at[j - 2], me.mate).wait_send()
-
-            R.sb[j % 2, 0] = self.part(k, 0).astype(bf16)
-            R.sb[j % 2, 1] = self.part(k, 1).astype(bf16)
-            self.copy(j, R.sb.at[j % 2], R.rb.at[j], me.mate).start()
-
-    def second(self):
-        me, R = self.me, self.R
-        if self.credit:
-            pl.semaphore_wait(R.free.at[1], 1)
-            pl.semaphore_wait(R.free.at[2], 1)
-
-        @pl.loop(0, 4)
-        def _(t):
-            dx, dy = 1 - t // 2, 1 - t % 2
-            xx = me.x + dx * (1 - 2 * me.x)
-            yy = me.y + dy * (1 - 2 * me.y)
-            j = xx * 2 + yy
-            k = me.index(xx, me.c, yy)
-            self.copy(j, R.sb.at[0], R.rb.at[j], me.mate).wait_recv()
-            R.rb[j, 0] = (self.part(k, 0) + R.rb[j, 0].astype(f32)).astype(bf16)
-            R.rb[j, 1] = (self.part(k, 1) + R.rb[j, 1].astype(f32)).astype(bf16)
-
-            @pl.when(t == 0)
+                self.for_mate(t)
+
+            @pl.when(t > 0)
             def _():
-                self.copy(4, R.rb.at[self.jd, 0], R.da, me.xn).start()
-                self.copy(5, R.rb.at[self.jd, 1], R.db, me.yn).start()
-
-            @pl.when(t == 1)
-            def _():
-                self.copy(6, R.rb.at[self.jx, 0], R.fx.at[0], me.xn).start()
-
-            @pl.when(t == 2)
-            def _():
-                self.copy(9, R.rb.at[self.jy, 1], R.fy.at[1], me.yn).start()
+                self.for_this(t - 1)
+
+            beside(t)
 
     def relay(self):
         me, R = self.me, self.R
@@ -573,7 +586,7 @@
     def finish(self, release):
         me, R = self.me, self.R
         for i in (2, 3):
-            self.copy(i, R.sb.at[i % 2], R.rb.at[i], me.mate).wait_send()
+            self.copy(i, R.sb.at[0], R.sb.at[0], me.mate).wait_send()
         for i in range(4, 10):
             self.copy(i, R.da, R.db, me.mate).wait_send()
         if release:
@@ -633,17 +646,26 @@
                 (R.wbc, stage(2 * C, 2 * C + BC)),
                 (R.wz, stage(0, C)),
                 (R.gcot, R.cot.at[aligned(me.q * SPAN, SPAN), :]),
+                (R.wo, R.wo_own),
+                (R.hidden_in, R.hid),
             )
         )
     ]
-    for copy in arriving:
+    little = [
+        pltpu.make_async_copy(getattr(R, "in_" + k), getattr(R, k), R.loc.at[12 + i])
+        for i, k in enumerate(LITTLE)
+    ]
+    for copy in arriving + little:
         copy.start()
     barrier = pltpu.get_barrier_semaphore()
     for d in range(1, 8):
         pl.semaphore_signal(barrier, 1, device_id=me.plane(d)[1], device_id_type=MESH)
     for d in range(1, n):
         pl.semaphore_signal(barrier, 1, device_id=me.line(d)[1], device_id_type=MESH)
+    for copy in little:
+        copy.wait()
     R.gains[...] = R.gain[...].reshape(1, D)
+    arriving[5].wait()
 
     @over(SPAN // 32)
     def _(i):
@@ -655,7 +677,7 @@
         copy.wait()
     R.wd[share(dp), C : 2 * C] = R.y[0:DS, C : 2 * C].astype(bf16)
     R.wd[share(dp), half] = R.y[0:DS, half].astype(bf16)
-    R.wdt[dp] = jnp.concatenate([R.w_dt[...], jnp.zeros((DS, 128 - H), f32)], axis=1).T[0:16, :].astype(bf16)
+    R.wdt[dp] = jnp.concatenate([R.w_dt[...], jnp.zeros((16 - H, DS), f32)], axis=0).astype(bf16)
     pl.semaphore_wait(barrier, 7 + n - 1)
 
     tokens = PlaneGather(me, R.hn, R.ag_s.at[0], R.ag_r.at[0])
@@ -673,10 +695,10 @@
     for g in gathers[:3]:
         g.start()
 
-    for copy in arriving[2:]:
+    for copy in arriving[2:5]:
         copy.wait()
     R.wd[share(dp), 0:C] = R.y[0:DS, 0:C].astype(bf16)
-    R.wot[share(dp), :] = R.wo[...].T.astype(bf16)
+    R.wot[share(dp), :] = R.wo_own[...].T.astype(bf16)
     own = aligned(me.q * C, C)
     taps = [R.conv_x[:, own]]
     for v in (R.conv_xb, R.gate):
@@ -788,19 +810,23 @@
         some = aligned(i * 256, 256)
         R.won[some, :] = nn(R.gg[...], R.cot[:, some]).astype(bf16).T
 
-    steps[1]()
-
     def scatter(i, src, lanes):
         slot = lambda k: (R.cot, (share(k), slice(*lanes)))
         return LineScatter(me, src, slot, R.zr_s.at[i], R.zr_r.at[i])
 
-    wo_sum = scatter(0, lambda k: (R.won, (share(k), slice(0, C))), (2 * C + 128, 3 * C + 128))
-    x_sum = scatter(1, lambda k: (R.wd, (share(k), slice(C, 2 * C))), (C, 2 * C))
+    wo_slot = lambda k: (
+        R.dcat,
+        (pl.ds(pl.multiple_of(C + k // 5 * DS, 16), DS), aligned(k % 5 * C, C)),
+    )
+    wo_sum = LineScatter(me, lambda k: (R.won, (share(k), slice(0, C))), wo_slot, R.zr_s.at[0], R.zr_r.at[0])
+    x_sum = scatter(1, lambda k: (R.won, (share(k), slice(0, C))), (C, 2 * C))
     z_sum = scatter(2, lambda k: (R.wot, (share(k), slice(0, C))), (0, C))
-    bc_sum = scatter(3, lambda k: (R.wd, (share(k), half)), (2 * C, 2 * C + 128))
     dt_sum = LineScatter(
         me, lambda k: (R.gdt, (k,)), lambda k: (R.rdt, (k,)), R.zr_s.at[4], R.zr_r.at[4]
     )
+    wo_steps = line(wo_sum.slot_step)
+    steps[1]()
+    wo_steps[0]()
     steps[2]()
     for k in range(0, D, 256):
         R.wout[:, k : k + 256] = R.wot[k : k + 256, :].T
@@ -830,19 +856,8 @@
         lambda k, h: nn(R.wot[dhalf(h), :], R.gg[:, aligned(k * SPAN, SPAN)]),
         False,
     )
-    mixed.first()
-
-    @pl.when(dp > 0)
-    def _():
-        pl.semaphore_wait(R.free.at[3], 1)
-
-    @pl.when(dp < n - 1)
-    def _():
-        pl.semaphore_wait(R.free.at[4], 1)
-
-    wo_steps = line(wo_sum.slot_step)
-    wo_steps[0]()
-    mixed.second()
+    wo_steps[1]()
+    mixed.blocks(lambda t: beside(t, {3: [wo_steps[2]]}))
     total_sums(1)
 
     @over(nb)
@@ -856,15 +871,25 @@
             g = nn(R.dcat[a:z, :], R.hn[:, some])
             R.ng[:, some] += jnp.sum(g * R.wcat[a:z, some].astype(f32), axis=0, keepdims=True)
             g = g.astype(bf16)
-            if z - a > 256:
-                R.gdt_all[:, some] = g[z - a - 16 : z - a]
-            w = min(z - a, 256)
+            w = z - a
+            if z == rows:
+                w -= 16
+                R.gdt_all[:, some] = g[w:]
             dst[some, at : at + w] = g[0:w].T
 
     R.ng[...] = jnp.zeros_like(R.ng)
-    weight_grad(0, 256, R.wot, 0)
-    weight_grad(256, C, R.wot, 256)
-    wo_steps[1]()
+    weight_grad(0, C, R.wot, 0)
+
+    @pl.when(dp > 0)
+    def _():
+        pl.semaphore_wait(R.free.at[3], 1)
+
+    @pl.when(dp < n - 1)
+    def _():
+        pl.semaphore_wait(R.free.at[4], 1)
+
+    z_steps = line(z_sum.slot_step)
+    z_steps[0]()
 
     def put(ref):
         def f(v, new):
@@ -875,7 +900,21 @@
 
         return f
 
-    out_copy = pltpu.make_async_copy(R.wout.at[0:SPAN, :], R.block_out, R.loc.at[5])
+    out_copy = pltpu.make_async_copy(R.wout.at[0:SPAN, :], R.out_block, R.loc.at[6])
+
+    leaving = [
+        pltpu.make_async_copy(a, b, R.loc.at[i])
+        for i, (a, b) in enumerate(
+            (
+                (R.gwo, R.out_wo),
+                (R.gz, R.out_z),
+                (R.gbc, R.out_bc),
+                (R.gx, R.out_x),
+                (R.small, R.out_small),
+                (R.gdt_out, R.out_dt),
+            )
+        )
+    ]
 
     def finish_mixed():
         def put(k, v):
@@ -886,19 +925,36 @@
         out_copy.start()
         mixed.finish(True)
 
+    wo_sum.total(put(R.gwo))
+    leaving[0].start()
+    for s in line(wo_sum.finish):
+        s()
     R.state[...] = jnp.zeros_like(R.state)
-    z_steps = line(z_sum.slot_step)
-    polls = {
-        0: [mixed.relay],
-        1: [wo_steps[2], z_steps[0]],
-        4: [z_steps[1], finish_mixed],
-        7: [z_steps[2]],
-    }
+    polls = {0: [mixed.relay], 2: [z_steps[1]], 5: [z_steps[2]]}
 
     @over(nb)
     def _(i):
         bwd_block(nb - 1 - i, R, offs, C, H)
         beside(i, polls)
+
+    weight_grad(2 * C, rows, R.cot, 2 * C + 128)
+    finish_mixed()
+    for k in range(n):
+        R.gdt[k] = R.gdt_all[:, k * DS : (k + 1) * DS]
+    bx = R.cot.at[0:D, 2 * C + 384 : 2 * C + 512]
+    bc_own = aligned(2 * C + 128 + me.c * 128, 128)
+    bc_other = aligned(2 * C + 256 - me.c * 128, 128)
+    bc_pair = remote(R.cot.at[0:D, bc_other], bx, R.mate_s.at[1], R.mate_r.at[1], me.mate)
+    bc_sum = scatter(3, lambda k: (R.cot, (share(k), bc_own)), (2 * C, 2 * C + 128))
+    bc_steps = line(bc_sum.slot_step, dt_sum.slot_step)
+    x_steps = line(x_sum.slot_step)
+    pl.semaphore_wait(R.free.at[0], 1)
+    bc_pair.start()
+    weight_grad(C, 2 * C, R.won, 0)
+    bc_pair.wait()
+    R.cot[0:D, bc_own] = (R.cot[0:D, bc_own].astype(f32) + bx[...].astype(f32)).astype(bf16)
+    bc_steps[0]()
+    x_steps[0]()
 
     dhn = PlaneScatter(
         me,
@@ -908,20 +964,7 @@
         lambda k, h: nn(R.wd[dhalf(h), 0:rows], R.dcat[:, aligned(k * SPAN, SPAN)]),
         True,
     )
-    dhn.first()
-    dhn.second()
-
-    weight_grad(2 * C - 256, 2 * C, R.wd, 2 * C - 256)
-    weight_grad(C, 2 * C - 256, R.wd, C)
-    x_steps = line(x_sum.slot_step)
-    x_steps[0]()
-    weight_grad(2 * C, rows, R.wd, 2 * C)
-    for k in range(n):
-        R.gdt[k] = R.gdt_all[:, k * DS : (k + 1) * DS]
-    bx = R.cot.at[0:D, 3 * C + 128 : 3 * C + 256]
-    bc_pair = remote(R.wd.at[:, other], bx, R.mate_s.at[1], R.mate_r.at[1], me.mate)
-    bc_pair.start()
-    dhn.relay()
+    dhn.blocks(lambda t: beside(t, {2: [bc_steps[1]], 4: [bc_steps[2], x_steps[1]]}))
 
     ax = [jnp.sum(R.accx[k], axis=1, keepdims=True) for k in range(7)]
     ab = [jnp.sum(R.accbc[k], axis=1, keepdims=True) for k in range(5)]
@@ -941,11 +984,25 @@
         k, device = me.line(d)
         remote(R.sv, R.lslot.at[dp], R.ls_s.at[k], R.ls_r.at[dp], device).start()
     R.lslot[dp] = R.sv[...]
-    x_steps[1]()
-    bc_pair.wait()
-    R.wd[:, half] = (R.wd[:, half].astype(f32) + bx[...].astype(f32)).astype(bf16)
-    bc_steps = line(bc_sum.slot_step, dt_sum.slot_step)
-    bc_steps[0]()
+    bc_sum.total(put(R.bsum))
+    j = me.x * 2 + me.y
+    R.bslot[j] = R.bsum[...].astype(bf16)
+    crossing = []
+    for i, (device, k) in enumerate(
+        ((me.xn, (1 - me.x) * 2 + me.y), (me.yn, me.x * 2 + 1 - me.y), (me.diag, (1 - me.x) * 2 + 1 - me.y))
+    ):
+        remote(R.bslot.at[j], R.bslot.at[j], R.bc_s.at[i], R.bc_r.at[i], device).start()
+        crossing.append(remote(R.bslot.at[k], R.bslot.at[k], R.bc_s.at[i], R.bc_r.at[i], device))
+    x_steps[2]()
+    dhn.relay()
+    for c in crossing:
+        c.wait()
+    v = R.bslot[0].astype(f32)
+    for k in range(1, 4):
+        v = v + R.bslot[k].astype(f32)
+    R.bfin[me.c] = v.astype(bf16)
+    bc_last = remote(R.bfin.at[me.c], R.bfin.at[me.c], R.mate_s.at[2], R.mate_r.at[2], me.mate)
+    bc_last.start()
     for d in range(1, n):
         k, device = me.line(d)
         remote(R.sv, R.lslot.at[k], R.ls_s.at[k], R.ls_r.at[k], device).wait()
@@ -957,33 +1014,20 @@
         k, device = me.plane(d)
         remote(R.pv, R.small.at[me.q], R.ps_s.at[k], R.ps_r.at[me.q], device).start()
     R.small[me.q] = total
-    bc_steps[1]()
-    x_steps[2]()
-    bc_steps[2]()
-
-    wo_sum.total(put(R.gwo))
     z_sum.total(put(R.gz))
-    bc_sum.total(put(R.bsum))
-    j = me.x * 2 + me.y
-    R.bslot[j] = R.bsum[...].astype(bf16)
-    crossing = []
-    for i, (device, k) in enumerate(
-        ((me.xn, (1 - me.x) * 2 + me.y), (me.yn, me.x * 2 + 1 - me.y), (me.diag, (1 - me.x) * 2 + 1 - me.y))
-    ):
-        remote(R.bslot.at[j], R.bslot.at[j], R.bc_s.at[i], R.bc_r.at[i], device).start()
-        crossing.append(remote(R.bslot.at[k], R.bslot.at[k], R.bc_s.at[i], R.bc_r.at[i], device))
+    leaving[1].start()
+    dt_sum.total(put(R.gdt_out))
+    bc_last.wait_send()
+    remote(
+        R.bfin.at[1 - me.c], R.bfin.at[1 - me.c], R.mate_s.at[2], R.mate_r.at[2], me.mate
+    ).wait_recv()
+    R.gbc[:, 0:128] = R.bfin[0].astype(f32)
+    R.gbc[:, 128:256] = R.bfin[1].astype(f32)
+    leaving[2].start()
     x_sum.total(put(R.gx))
-    dt_sum.total(put(R.gdt_out))
-    for c in crossing:
-        c.wait()
-    v = R.bslot[0].astype(f32)
-    for k in range(1, 4):
-        v = v + R.bslot[k].astype(f32)
-    R.bfin[me.c] = v.astype(bf16)
-    bc_last = remote(R.bfin.at[me.c], R.bfin.at[me.c], R.mate_s.at[2], R.mate_r.at[2], me.mate)
-    bc_last.start()
-
-    cot_again = pltpu.make_async_copy(R.gcot, R.hn.at[0:SPAN, :], R.loc.at[4])
+    leaving[3].start()
+
+    cot_again = pltpu.make_async_copy(R.gcot, R.hn.at[0:SPAN, :], R.loc.at[11])
     cot_again.start()
 
     def put_dh(k, v):
@@ -1003,60 +1047,60 @@
             R.hn[some, :].astype(f32) + qn * w - u * (qn * qn * qn * dot)
         ).astype(bf16)
 
-    in_copy = pltpu.make_async_copy(R.hn.at[SPAN : 2 * SPAN, :], R.grad_in, R.loc.at[6])
+    in_copy = pltpu.make_async_copy(R.hn.at[SPAN : 2 * SPAN, :], R.out_grad, R.loc.at[7])
     in_copy.start()
-    bc_last.wait_send()
-    remote(
-        R.bfin.at[1 - me.c], R.bfin.at[1 - me.c], R.mate_s.at[2], R.mate_r.at[2], me.mate
-    ).wait_recv()
-    R.gbc[:, 0:128] = R.bfin[0].astype(f32)
-    R.gbc[:, 128:256] = R.bfin[1].astype(f32)
     for d in range(1, 8):
         k, device = me.plane(d)
         remote(R.pv, R.small.at[k], R.ps_s.at[k], R.ps_r.at[k], device).wait()
+    leaving[4].start()
+    leaving[5].start()
     dhn.finish(False)
-    for fin in (wo_sum, x_sum, z_sum, bc_sum, dt_sum):
+    for fin in (x_sum, z_sum, bc_sum, dt_sum):
         for s in line(fin.finish):
             s()
     in_copy.wait()
     out_copy.wait()
+    for copy in leaving:
+        copy.wait()
 
 
 def unpack(names, C, H, *refs):
     R = types.SimpleNamespace(**dict(zip(names, refs)))
-    big = [
-        pltpu.make_async_copy(a, b, R.sem.at[i])
-        for i, (a, b) in enumerate(
-            (
-                (R.block_out, R.o_block),
-                (R.grad_in, R.o_grad),
-                (R.gz, R.o_z),
-                (R.gx, R.o_x),
-                (R.gbc, R.o_bc),
-            )
-        )
-    ]
-    for copy in big:
+    ins = ("small", "dt", "wo", "z", "x", "bc", "block", "grad")
+    come = [pltpu.make_async_copy(getattr(R, "out_" + k), getattr(R, "v_" + k), R.sem.at[i]) for i, k in enumerate(ins)]
+    outs = [k for k in names if k.startswith("o_")]
+    there = dict(o_z="v_z", o_x="v_x", o_bc="v_bc", o_block="v_block", o_grad="v_grad")
+    go = {
+        k: pltpu.make_async_copy(getattr(R, there.get(k, "s_" + k)), getattr(R, k), R.sem.at[len(ins) + i])
+        for i, k in enumerate(outs)
+    }
+    for copy in come:
         copy.start()
-    R.o_wo[...] = R.gwo[...].T
-    DS = R.gdt_out.shape[1]
-    R.o_dt[...] = jnp.concatenate([R.gdt_out[...], jnp.zeros((112, DS), f32)], axis=0).T[:, 0:H]
-    row = lambda k: jnp.concatenate([R.small[q, k : k + 1, :] for q in range(8)], axis=1)
+    come[0].wait()
+    row = lambda k: jnp.concatenate([R.v_small[q, k : k + 1, :] for q in range(8)], axis=1)
     for k in range(KERNEL):
-        R.o_cx[k : k + 1, :] = row(k)
-    R.o_cxb[...] = row(4).reshape(8 * C)
-    R.o_gate[...] = row(5).reshape(8 * C)
-    for ref, at in ((R.o_dtb, 0), (R.o_alog, 8), (R.o_skip, 16)):
-        v = jnp.concatenate([R.small[q, 6:7, at : at + H] for q in range(8)], axis=1)
+        R.s_o_cx[k : k + 1, :] = row(k)
+    R.s_o_cxb[...] = row(4).reshape(8 * C)
+    R.s_o_gate[...] = row(5).reshape(8 * C)
+    for ref, at in ((R.s_o_dtb, 0), (R.s_o_alog, 8), (R.s_o_skip, 16)):
+        v = jnp.concatenate([R.v_small[q, 6:7, at : at + H] for q in range(8)], axis=1)
         ref[...] = v.reshape(8 * H)
-    total = R.small[0, 8:24, :]
+    total = R.v_small[0, 8:24, :]
     for q in range(1, 8):
-        total = total + R.small[q, 8:24, :]
-    R.o_cbc[...] = total[0:KERNEL, 0:BC]
-    R.o_cbcb[...] = total[4:5, 0:BC].reshape(BC)
+        total = total + R.v_small[q, 8:24, :]
+    R.s_o_cbc[...] = total[0:KERNEL, 0:BC]
+    R.s_o_cbcb[...] = total[4:5, 0:BC].reshape(BC)
     D = R.o_ng.shape[0]
-    R.o_ng[...] = jnp.concatenate([total[8 + k : 9 + k, :] for k in range(D // C)], axis=1).reshape(D)
-    for copy in big:
+    R.s_o_ng[...] = jnp.concatenate([total[8 + k : 9 + k, :] for k in range(D // C)], axis=1).reshape(D)
+    come[1].wait()
+    R.s_o_dt[...] = R.v_dt[0:H, :]
+    come[2].wait()
+    R.s_o_wo[...] = R.v_wo[...].T
+    for copy in come[3:]:
+        copy.wait()
+    for copy in go.values():
+        copy.start()
+    for copy in go.values():
         copy.wait()
 
 
@@ -1089,36 +1133,45 @@
     nb = T // SPAN
     wide_rows = 2 * C + BC + 16
     inputs = dict(
-        hid=hidden_in,
+        hidden_in=hidden_in,
         gcot=grad_out,
         wz=w_z,
         wx=w_x,
         wbc=w_bc,
-        w_dt=w_dt,
+        in_w_dt=w_dt.T,
         wo=w_out,
-        gain=norm_gain,
-        conv_x=conv_x,
-        conv_xb=conv_x_bias,
-        conv_bc=conv_bc,
-        conv_bcb=conv_bc_bias,
-        dt_bias=dt_bias,
-        a_log=a_log,
-        skip=skip_d,
-        gate=gate_gain,
+        in_gain=norm_gain,
+        in_conv_x=conv_x,
+        in_conv_xb=conv_x_bias,
+        in_conv_bc=conv_bc,
+        in_conv_bcb=conv_bc_bias,
+        in_dt_bias=dt_bias,
+        in_a_log=a_log,
+        in_skip=skip_d,
+        in_gate=gate_gain,
         lengths=lengths,
         perm=perm,
     )
     outputs = dict(
-        block_out=((rows, D), bf16),
-        grad_in=((rows, D), bf16),
+        out_block=((rows, D), bf16),
+        out_grad=((rows, D), bf16),
+        out_dt=((16, DS), f32),
+        out_z=((DS, C), f32),
+        out_x=((DS, C), f32),
+        out_bc=((DS, BC), f32),
+        out_wo=((DS, C), f32),
+        out_small=((8, 24, C), f32),
+    )
+    scratch = dict(
+        **{k: (inputs["in_" + k].shape, f32) for k in LITTLE},
+        hid=((rows, D), bf16),
+        wo_own=((C, DS), f32),
+        gdt_out=((16, DS), f32),
         gz=((DS, C), f32),
         gx=((DS, C), f32),
         gbc=((DS, BC), f32),
-        gdt_out=((16, DS), f32),
         gwo=((DS, C), f32),
         small=((8, 24, C), f32),
-    )
-    scratch = dict(
         hn=((T, D), bf16),
         cot=((T, D), bf16),
         wd=((D, 2 * C + BC + 128), bf16),
@@ -1196,13 +1249,14 @@
         ps_r=(8,),
         bc_s=(3,),
         bc_r=(3,),
-        loc=(7,),
+        loc=(22,),
     )
     names = [*inputs, *outputs, *scratch, *semaphores, "free"]
     vmem = pl.BlockSpec(memory_space=pltpu.VMEM)
     hbm = pl.BlockSpec(memory_space=pl.ANY)
     smem = pl.BlockSpec(memory_space=pltpu.SMEM)
-    where = {k: hbm for k in ("gcot", "wz", "wx", "wbc", "block_out", "grad_in")}
+    where = {k: hbm for k in ("hidden_in", "gcot", "wz", "wx", "wbc", "wo", *outputs)}
+    where.update({"in_" + k: hbm for k in LITTLE})
     where.update(lengths=smem, perm=smem)
     out = pl.pallas_call(
         functools.partial(kernel, names, n, C, H),
@@ -1223,7 +1277,7 @@
         o_ng=((D,), f32),
         o_z=((DS, C), f32),
         o_x=((DS, C), f32),
-        o_dt=((DS, H), f32),
+        o_dt=((H, DS), f32),
         o_bc=((DS, BC), f32),
         o_cx=((KERNEL, inner), f32),
         o_cxb=((inner,), f32),
@@ -1235,15 +1289,17 @@
         o_gate=((inner,), f32),
         o_wo=((C, DS), f32),
     )
-    copied = ("o_block", "o_grad", "o_z", "o_x", "o_bc")
-    place = lambda k: hbm if k in copied else vmem
-    return pl.pallas_call(
-        functools.partial(unpack, [*outputs, *results, "sem"], C, H),
+    held = {"v_" + k[4:]: v for k, v in outputs.items()}
+    held.update({"s_" + k: v for k, v in results.items() if "v_" + k[2:] not in held or k in ("o_dt", "o_wo")})
+    made = pl.pallas_call(
+        functools.partial(unpack, [*outputs, *results, *held, "sem"], C, H),
         out_shape=[jax.ShapeDtypeStruct(*s) for s in results.values()],
-        in_specs=[place(k) for k in outputs],
-        out_specs=[place(k) for k in results],
-        scratch_shapes=[pltpu.SemaphoreType.DMA((5,))],
+        in_specs=[hbm] * len(outputs),
+        out_specs=[hbm] * len(results),
+        scratch_shapes=[pltpu.VMEM(*s) for s in held.values()]
+        + [pltpu.SemaphoreType.DMA((len(outputs) + len(results),))],
     )(*out)
+    return tuple(v.T if k == "o_dt" else v for k, v in zip(results, made))
 
 
 def solution(mesh):

time: 197 us -> 181 us (0.919)
  Pallas kernels: 192 us -> 179 us
  local copies, waits for them, and re-layouts: 3.16 us -> 0 us
    pallas_call x1, Pallas kernels: 187 us -> 175 us  [shards(): pl.pallas_call(functools.partial(kernel, names, n, C, H), out_shape=[jax....]
where the time goes in v3:
time: 181 us; the launch traced here: 180 us
  Pallas kernels  179 us (99%)
    pallas_call x1, Pallas kernels, shards(): pl.pallas_call(functools.partial(kernel, names, n, C, H), out_shape=[jax....  175 us
    pallas_call x1, Pallas kernels, shards(): pl.pallas_call(functools.partial(unpack, [*outputs, *results, *held, 'sem...  4.25 us

profile of v3, /device:TPU:8, one launch (start us, length us, event | category | flops | bytes accessed | tf_op | source)
XLA Modules:
  0.0 180.3 jit_solution(16821904522968745011)
XLA Ops:
  0.7 175.2 %shard_map.297 = (bf16[256,1536]{1,0:T(8,128)(2,1)}, bf16[256,1536]{1,0:T(8,128)(2,1)}, f32[16,384]{1,0:T(8,128)}, f32[384,384]{1,0:T(8,128)}, f32[384,384]{1,0:...) custom-call(bf16[256,1536]{1,0:T(8,128)(2,1)} %refs_0_.1, bf16[256,1536]{1,0:T(8,128)(2,1)} %refs_1_.1, ...), custom_call_target="tpu_custom_call" | custom-call | tf_op jit(solution)/shard_map/pallas_call | solution.py:1261
  175.9 4.3 %shard_map.298 = (bf16[256,1536]{1,0:T(8,128)(2,1)}, bf16[256,1536]{1,0:T(8,128)(2,1)}, f32[1536]{0:T(1024)}, f32[384,384]{1,0:T(8,128)}, f32[384,384]{1,0:T(8,1...) custom-call(bf16[256,1536]{1,0:T(8,128)(2,1)} %get-tuple-element.40., ...), custom_call_target="tpu_custom_call" | custom-call | tf_op jit(solution)/shard_map/pallas_call | solution.py:1294
